TPU v7x, 32 devices: a whole 2x2x4 slice. The times are simulated.
32 devices in a mesh: tok: 8 (over z, x), dim: 4 (over y, core).
Axes of the slice: x: 2, y: 2, z: 4, core: 2. Of those that a mesh axis runs over, the one named last changes fastest.
Arguments:
- inputs: bfloat16 [16384, 1024], P('tok', 'dim'), may hold values from -9 to 9
- cotangent: bfloat16 [16384, 1024], P('tok', 'dim'), may hold values from -6 to 6
- lengths: int32 [8, 3], P('tok'), may hold values from 1 to 1024, 2048 in all within a row
- pad_mask: int32 [16384], P('tok'), may hold values 0 or 1
- attention_weights: float32 [4, 1024, 1024], P(None, 'dim', 'tok'), may hold values from -5.8 to 5.8
- gated_weights: float32 [3, 4096, 1024], P(None, 'dim', 'tok'), may hold values from -5.8 to 5.8
- model_gains: float32 [3, 1024], P(None, 'dim'), may hold values from 0.1 to 1.8
- unit_gains: float32 [2, 4096], P(None, 'dim'), may hold values from 0.5 to 1.5
- attention_moment: float32 [4, 1024, 1024], P(None, 'dim', 'tok'), may hold values from -6 to 6
- attention_square: float32 [4, 1024, 1024], P(None, 'dim', 'tok'), may hold values from 1.44 to 5.76
- gated_moment: float32 [3, 4096, 1024], P(None, 'dim', 'tok'), may hold values from -6 to 6
- gated_square: float32 [3, 4096, 1024], P(None, 'dim', 'tok'), may hold values from 1.44 to 5.76
- model_moment: float32 [3, 1024], P(None, 'dim'), may hold values from -384 to 384
- model_square: float32 [3, 1024], P(None, 'dim'), may hold values from 4096 to 16384
- unit_moment: float32 [2, 4096], P(None, 'dim'), may hold values from -384 to 384
- unit_square: float32 [2, 4096], P(None, 'dim'), may hold values from 4096 to 16384
Outputs:
- layer_out: bfloat16 [16384, 1024], P('tok', 'dim')
- input_gradient: float32 [16384, 1024], P('tok', 'dim')
- attention_next: float32 [4, 1024, 1024], P(None, 'dim', 'tok')
- attention_copy: bfloat16 [4, 1024, 1024], P(None, 'dim', 'tok')
- moment_attention: float32 [4, 1024, 1024], P(None, 'dim', 'tok')
- square_attention: float32 [4, 1024, 1024], P(None, 'dim', 'tok')
- gated_next: float32 [3, 4096, 1024], P(None, 'dim', 'tok')
- gated_copy: bfloat16 [3, 4096, 1024], P(None, 'dim', 'tok')
- moment_gated: float32 [3, 4096, 1024], P(None, 'dim', 'tok')
- square_gated: float32 [3, 4096, 1024], P(None, 'dim', 'tok')
- model_next: float32 [3, 1024], P(None, 'dim')
- moment_model: float32 [3, 1024], P(None, 'dim')
- square_model: float32 [3, 1024], P(None, 'dim')
- unit_next: float32 [2, 4096], P(None, 'dim')
- moment_unit: float32 [2, 4096], P(None, 'dim')
- square_unit: float32 [2, 4096], P(None, 'dim')
- gradient_norm: float32 [1], replicated
- mean_alpha: float32 [2], replicated
Inputs may be any that keep to these rules, and one draw needn't show every extreme that they name: Each pack's 3 lengths add up to 2048.
All inputs are finite; a program needn't handle non-finite values. No bound on the sum of `pad_mask` on one device may be relied on, other than what follows from the above.
Results may differ from a plain program's by a relative error of at most 0.01.
The roundings to bfloat16 on the way count: a program that leaves them out, or rounds other values in their place, can miss the bound.
Values may be sent and summed in bfloat16 or wider, within the bound.
No kernel may reach another device: no remote copies, remote signals or barrier semaphores. Data moves between devices by JAX's collectives and lax.ppermute only.
A program may use at most 192 MiB of HBM per device.

v0:
```python
import jax
import jax.numpy as jnp
from jax import lax
from jax.sharding import PartitionSpec as P

D = 1024
HEAD = 64
FF = 4096
STEP = 4
QBLK = 512


EPSILON = 1e-06
ADAM_EPSILON = 1e-08
BETA_ONE = 0.5
BETA_TWO = 0.5
LEARN_RATE = 1.5
MASKED_SCORE = -1e30


def token_sum(local_sum):
    return lax.psum(local_sum, "dim")


def whole_rows(shard):
    return lax.all_gather(shard, "dim", axis=1, tiled=True)


def own_rows(partial_value):
    return lax.psum_scatter(partial_value, "dim", scatter_dimension=1, tiled=True)


def branch_rows(low_rows, weight_rows, scale_value):
    return own_rows(
        jnp.einsum("tr,rd->td", low_rows, weight_rows, preferred_element_type=jnp.float32)
        * scale_value
    )


def sphere(values):
    square_total = token_sum(jnp.sum(values * values, axis=1))
    factor = lax.rsqrt(square_total / D + EPSILON)
    return (values * factor[:, None], factor)


def sphere_back(delta_unit, unit, factor):
    inner_mean = token_sum(jnp.sum(delta_unit * unit, axis=1)) / D
    return factor[:, None] * (delta_unit - unit * inner_mean[:, None])


def blend(residual, branch, alpha_gain):
    branch_unit, branch_factor = sphere(branch)
    mixed_rows = residual + alpha_gain * (branch_unit - residual)
    mixed_unit, mixed_factor = sphere(mixed_rows)
    return (branch_unit, branch_factor, mixed_unit, mixed_factor)


def head_sphere(values, heads_here):
    row_count = values.shape[0]
    split_rows = values.reshape(row_count, heads_here, HEAD)
    factor = lax.rsqrt(jnp.mean(split_rows * split_rows, axis=2) + EPSILON)
    return ((split_rows * factor[:, :, None]).reshape(row_count, -1), factor)


def head_back(delta_unit, unit, factor):
    row_count, heads_here = factor.shape
    delta_split = delta_unit.reshape(row_count, heads_here, HEAD)
    unit_split = unit.reshape(row_count, heads_here, HEAD)
    inner_mean = jnp.mean(delta_split * unit_split, axis=2)
    return (factor[:, :, None] * (delta_split - unit_split * inner_mean[:, :, None])).reshape(
        row_count, -1
    )


def to_heads(values, heads_here):
    row_count = values.shape[0]
    return values.reshape(row_count, heads_here, HEAD).transpose(1, 0, 2)


def from_heads(values):
    heads_here, row_count, head_width = values.shape
    return values.transpose(1, 0, 2).reshape(row_count, heads_here * head_width)


def visible(first_row, segment, padding):
    places = jnp.arange(segment.shape[0], dtype=jnp.int32)
    row_ids = first_row + jnp.arange(QBLK, dtype=jnp.int32)
    segment_rows = lax.dynamic_slice_in_dim(segment, first_row, QBLK, 0)
    same_seq = segment_rows[:, None] == segment[None, :]
    before = places[None, :] <= row_ids[:, None]
    live_key = (padding[None, :] == 1) | (places[None, :] == row_ids[:, None])
    return same_seq & before & live_key


def attend_heads(query_heads, key_heads, value_heads, segment, padding):
    token_count = segment.shape[0]
    first_rows = jnp.arange(token_count // QBLK, dtype=jnp.int32) * QBLK
    scale_head = HEAD ** (-0.5)

    def one_head(pieces):
        query_head, key_head, value_head = pieces

        def one_block(first_row):
            query_rows = lax.dynamic_slice_in_dim(query_head, first_row, QBLK, 0)
            raw_scores = (
                jnp.einsum("qe,ke->qk", query_rows, key_head, preferred_element_type=jnp.float32)
                * scale_head
            )
            scores = jnp.where(visible(first_row, segment, padding), raw_scores, MASKED_SCORE)
            row_max = jnp.max(scores, axis=1, keepdims=True)
            exponents = jnp.exp(scores - row_max)
            row_total = jnp.sum(exponents, axis=1, keepdims=True)
            probs_low = (exponents / row_total).astype(jnp.bfloat16)
            mixed_rows = jnp.einsum(
                "qk,ke->qe", probs_low, value_head, preferred_element_type=jnp.float32
            )
            return (mixed_rows, (row_max + jnp.log(row_total))[:, 0])

        mixed_heads, log_totals = lax.map(one_block, first_rows)
        return (mixed_heads.reshape(token_count, HEAD), log_totals.reshape(token_count))

    return lax.map(one_head, (query_heads, key_heads, value_heads))


def attend_back(query_heads, key_heads, value_heads, delta_heads, log_totals, segment, padding):
    token_count = segment.shape[0]
    first_rows = jnp.arange(token_count // QBLK, dtype=jnp.int32) * QBLK
    scale_head = HEAD ** (-0.5)

    def one_head(pieces):
        query_head, key_head, value_head, delta_head, log_total = pieces

        def one_block(running, first_row):
            key_acc, value_acc = running
            query_rows = lax.dynamic_slice_in_dim(query_head, first_row, QBLK, 0)
            delta_rows = lax.dynamic_slice_in_dim(delta_head, first_row, QBLK, 0)
            log_rows = lax.dynamic_slice_in_dim(log_total, first_row, QBLK, 0)
            raw_scores = (
                jnp.einsum("qe,ke->qk", query_rows, key_head, preferred_element_type=jnp.float32)
                * scale_head
            )
            scores = jnp.where(visible(first_row, segment, padding), raw_scores, MASKED_SCORE)
            probs_rows = jnp.exp(scores - log_rows[:, None])
            delta_probs = jnp.einsum(
                "qe,ke->qk", delta_rows, value_head, preferred_element_type=jnp.float32
            )
            inner_sum = jnp.sum(probs_rows * delta_probs, axis=1, keepdims=True)
            delta_scores = (probs_rows * (delta_probs - inner_sum)).astype(jnp.bfloat16)
            delta_query = (
                jnp.einsum("qk,ke->qe", delta_scores, key_head, preferred_element_type=jnp.float32)
                * scale_head
            )
            key_acc = (
                key_acc
                + jnp.einsum(
                    "qk,qe->ke", delta_scores, query_rows, preferred_element_type=jnp.float32
                )
                * scale_head
            )
            value_acc = value_acc + jnp.einsum(
                "qk,qe->ke",
                probs_rows.astype(jnp.bfloat16),
                delta_rows,
                preferred_element_type=jnp.float32,
            )
            return ((key_acc, value_acc), delta_query)

        empty_acc = jnp.zeros((token_count, HEAD), jnp.float32)
        (delta_key, delta_value), delta_query = lax.scan(
            one_block, (empty_acc, empty_acc), first_rows
        )
        return (delta_query.reshape(token_count, HEAD), delta_key, delta_value)

    return lax.map(one_head, (query_heads, key_heads, value_heads, delta_heads, log_totals))


def moment_update(weights, gradient, moment, square, fix_first, fix_second):
    moment_next = BETA_ONE * moment + (1.0 - BETA_ONE) * gradient
    square_next = BETA_TWO * square + (1.0 - BETA_TWO) * gradient * gradient
    stepped = weights - LEARN_RATE * (moment_next / fix_first) / (
        jnp.sqrt(square_next / fix_second) + ADAM_EPSILON
    )
    return (stepped, moment_next, square_next)


def local(
    inputs,
    cotangent,
    lengths,
    pad_mask,
    attention_weights,
    gated_weights,
    model_gains,
    unit_gains,
    attention_moment,
    attention_square,
    gated_moment,
    gated_square,
    model_moment,
    model_square,
    unit_moment,
    unit_square,
):
    token_count, width_here = inputs.shape
    heads_here = width_here // HEAD
    hidden_here = gated_weights.shape[1]
    scale_model = D ** (-0.5)
    scale_hidden = FF ** (-0.5)
    length_row = lengths[0]
    pack_starts = jnp.cumsum(length_row) - length_row
    places = jnp.arange(token_count, dtype=jnp.int32)
    segment = jnp.sum((places[:, None] >= pack_starts[None, 1:]).astype(jnp.int32), axis=1)
    attention_low, gated_low = (
        lax.all_gather(attention_weights.astype(jnp.bfloat16), "tok", axis=2, tiled=True),
        lax.all_gather(gated_weights.astype(jnp.bfloat16), "tok", axis=2, tiled=True),
    )
    residual = inputs.astype(jnp.float32)
    tokens_all = whole_rows(inputs)
    projected = (
        jnp.einsum(
            "td,rd->tr",
            tokens_all,
            attention_low[:3].reshape(3 * width_here, D),
            preferred_element_type=jnp.float32,
        )
        * scale_model
    )
    queries = projected[:, :width_here]
    keys_full = projected[:, width_here : 2 * width_here]
    values_full = projected[:, 2 * width_here :]
    score_gain = model_gains[0]
    alpha_mixer = model_gains[1]
    alpha_gated = model_gains[2]
    query_unit, query_factor = head_sphere(queries, heads_here)
    key_unit, key_factor = head_sphere(keys_full, heads_here)
    query_low = (query_unit * score_gain).astype(jnp.bfloat16)
    key_low = (key_unit * score_gain).astype(jnp.bfloat16)
    value_low = values_full.astype(jnp.bfloat16)
    query_heads = to_heads(query_low, heads_here)
    key_heads = to_heads(key_low, heads_here)
    value_heads = to_heads(value_low, heads_here)
    mixed_heads, log_totals = attend_heads(query_heads, key_heads, value_heads, segment, pad_mask)
    mixed_low = from_heads(mixed_heads).astype(jnp.bfloat16)
    branch_mixer = branch_rows(mixed_low, attention_low[3], scale_model)
    mixer_unit, mixer_factor, hidden_one, one_factor = blend(residual, branch_mixer, alpha_mixer)
    hidden_all = whole_rows(hidden_one.astype(jnp.bfloat16))
    upward = (
        jnp.einsum("td,fd->tf", hidden_all, gated_low[0], preferred_element_type=jnp.float32)
        * scale_model
    )
    gating = (
        jnp.einsum("td,fd->tf", hidden_all, gated_low[1], preferred_element_type=jnp.float32)
        * scale_model
    )
    upward_scaled = unit_gains[0] * upward
    gating_scaled = unit_gains[1] * gating
    sigmoid_gate = jax.nn.sigmoid(gating_scaled)
    middle_low = (upward_scaled * gating_scaled * sigmoid_gate).astype(jnp.bfloat16)
    branch_gated = branch_rows(middle_low, gated_low[2], scale_hidden)
    gated_unit, gated_factor, layer_rows, layer_factor = blend(
        hidden_one, branch_gated, alpha_gated
    )
    attention_back, gated_back = (
        lax.all_gather(attention_weights.astype(jnp.bfloat16), "tok", axis=2, tiled=True),
        lax.all_gather(gated_weights.astype(jnp.bfloat16), "tok", axis=2, tiled=True),
    )
    seed_rows = cotangent.astype(jnp.float32) * pad_mask.astype(jnp.float32)[:, None]
    delta_layer = sphere_back(seed_rows, layer_rows, layer_factor)
    delta_alpha_gated = jnp.sum(delta_layer * (gated_unit - hidden_one), axis=0)
    delta_hidden = (1.0 - alpha_gated) * delta_layer
    delta_branch = sphere_back(alpha_gated * delta_layer, gated_unit, gated_factor)
    delta_gated_all = whole_rows(delta_branch.astype(jnp.bfloat16))
    delta_down = (
        jnp.einsum("tf,td->fd", middle_low, delta_gated_all, preferred_element_type=jnp.float32)
        * scale_hidden
    )
    delta_middle = (
        jnp.einsum("td,fd->tf", delta_gated_all, gated_back[2], preferred_element_type=jnp.float32)
        * scale_hidden
    )
    delta_upward = delta_middle * gating_scaled * sigmoid_gate
    delta_gating = (
        delta_middle * upward_scaled * sigmoid_gate * (1.0 + gating_scaled * (1.0 - sigmoid_gate))
    )
    delta_units = jnp.stack(
        [jnp.sum(delta_upward * upward, axis=0), jnp.sum(delta_gating * gating, axis=0)]
    )
    delta_expand_low = jnp.concatenate(
        [unit_gains[0] * delta_upward, unit_gains[1] * delta_gating], axis=1
    ).astype(jnp.bfloat16)
    delta_expand = (
        jnp.einsum("tr,td->rd", delta_expand_low, hidden_all, preferred_element_type=jnp.float32)
        * scale_model
    )
    delta_hidden = delta_hidden + own_rows(
        jnp.einsum(
            "tr,rd->td",
            delta_expand_low,
            gated_back[:2].reshape(2 * hidden_here, D),
            preferred_element_type=jnp.float32,
        )
        * scale_model
    )
    delta_one = sphere_back(delta_hidden, hidden_one, one_factor)
    delta_alpha_mixer = jnp.sum(delta_one * (mixer_unit - residual), axis=0)
    delta_inputs = (1.0 - alpha_mixer) * delta_one
    delta_mixer = sphere_back(alpha_mixer * delta_one, mixer_unit, mixer_factor)
    delta_mixer_all = whole_rows(delta_mixer.astype(jnp.bfloat16))
    delta_out_weight = (
        jnp.einsum("tr,td->rd", mixed_low, delta_mixer_all, preferred_element_type=jnp.float32)
        * scale_model
    )
    delta_mixed = (
        jnp.einsum(
            "td,rd->tr", delta_mixer_all, attention_back[3], preferred_element_type=jnp.float32
        )
        * scale_model
    ).astype(jnp.bfloat16)
    delta_query_heads, delta_key_heads, delta_value_heads = attend_back(
        query_heads,
        key_heads,
        value_heads,
        to_heads(delta_mixed, heads_here),
        log_totals,
        segment,
        pad_mask,
    )
    delta_query = from_heads(delta_query_heads)
    delta_key = from_heads(delta_key_heads)
    delta_values = from_heads(delta_value_heads)
    delta_scale = jnp.sum(delta_query * query_unit + delta_key * key_unit, axis=0)
    delta_queries = head_back(score_gain * delta_query, query_unit, query_factor)
    delta_keys = head_back(score_gain * delta_key, key_unit, key_factor)
    delta_project = jnp.concatenate([delta_queries, delta_keys, delta_values], axis=1).astype(
        jnp.bfloat16
    )
    delta_inward = (
        jnp.einsum("tr,td->rd", delta_project, tokens_all, preferred_element_type=jnp.float32)
        * scale_model
    )
    delta_inputs = delta_inputs + own_rows(
        jnp.einsum(
            "tr,rd->td",
            delta_project,
            attention_back[:3].reshape(3 * width_here, D),
            preferred_element_type=jnp.float32,
        )
        * scale_model
    )
    inward_grad, out_grad, expand_grad, down_grad = (
        lax.psum_scatter(delta_inward, "tok", scatter_dimension=1, tiled=True),
        lax.psum_scatter(delta_out_weight, "tok", scatter_dimension=1, tiled=True),
        lax.psum_scatter(delta_expand, "tok", scatter_dimension=1, tiled=True),
        lax.psum_scatter(delta_down, "tok", scatter_dimension=1, tiled=True),
    )
    attention_grad = jnp.concatenate(
        [inward_grad.reshape(3, width_here, -1), out_grad[None]], axis=0
    )
    gated_grad = jnp.concatenate([expand_grad.reshape(2, hidden_here, -1), down_grad[None]], axis=0)
    model_grad, unit_grad = lax.psum(
        (jnp.stack([delta_scale, delta_alpha_mixer, delta_alpha_gated]), delta_units), "tok"
    )
    fix_first = 1.0 - BETA_ONE**STEP
    fix_second = 1.0 - BETA_TWO**STEP
    attention_stepped, moment_attention, square_attention = moment_update(
        attention_weights, attention_grad, attention_moment, attention_square, fix_first, fix_second
    )
    gated_stepped, moment_gated, square_gated = moment_update(
        gated_weights, gated_grad, gated_moment, gated_square, fix_first, fix_second
    )
    model_next, moment_model, square_model = moment_update(
        model_gains, model_grad, model_moment, model_square, fix_first, fix_second
    )
    unit_next, moment_unit, square_unit = moment_update(
        unit_gains, unit_grad, unit_moment, unit_square, fix_first, fix_second
    )
    attention_rows, gated_rows = lax.psum(
        (
            jnp.sum(attention_stepped * attention_stepped, axis=2),
            jnp.sum(gated_stepped * gated_stepped, axis=2),
        ),
        "tok",
    )
    attention_next = attention_stepped * lax.rsqrt(attention_rows / D + EPSILON)[:, :, None]
    gated_next = gated_stepped * lax.rsqrt(gated_rows / D + EPSILON)[:, :, None]
    token_groups = lax.axis_size("tok")
    local_square = (
        jnp.sum(attention_grad * attention_grad)
        + jnp.sum(gated_grad * gated_grad)
        + (jnp.sum(model_grad * model_grad) + jnp.sum(unit_grad * unit_grad)) / token_groups
    )
    square_total, alpha_total = lax.psum(
        (local_square, jnp.sum(model_next[1:], axis=1) / token_groups), ("tok", "dim")
    )
    gradient_norm = jnp.sqrt(square_total).reshape(1)
    mean_alpha = alpha_total / D
    return (
        layer_rows.astype(jnp.bfloat16),
        delta_inputs,
        attention_next,
        attention_next.astype(jnp.bfloat16),
        moment_attention,
        square_attention,
        gated_next,
        gated_next.astype(jnp.bfloat16),
        moment_gated,
        square_gated,
        model_next,
        moment_model,
        square_model,
        unit_next,
        moment_unit,
        square_unit,
        gradient_norm,
        mean_alpha,
    )


def solution(mesh):
    in_specs = (
        P("tok", "dim"),
        P("tok", "dim"),
        P("tok", None),
        P("tok"),
        P(None, "dim", "tok"),
        P(None, "dim", "tok"),
        P(None, "dim"),
        P(None, "dim"),
        P(None, "dim", "tok"),
        P(None, "dim", "tok"),
        P(None, "dim", "tok"),
        P(None, "dim", "tok"),
        P(None, "dim"),
        P(None, "dim"),
        P(None, "dim"),
        P(None, "dim"),
    )
    out_specs = (
        P("tok", "dim"),
        P("tok", "dim"),
        P(None, "dim", "tok"),
        P(None, "dim", "tok"),
        P(None, "dim", "tok"),
        P(None, "dim", "tok"),
        P(None, "dim", "tok"),
        P(None, "dim", "tok"),
        P(None, "dim", "tok"),
        P(None, "dim", "tok"),
        P(None, "dim"),
        P(None, "dim"),
        P(None, "dim"),
        P(None, "dim"),
        P(None, "dim"),
        P(None, "dim"),
        P(),
        P(),
    )
    return jax.shard_map(local, mesh=mesh, in_specs=in_specs, out_specs=out_specs, check_vma=False)
```

profile of v0, /device:TPU:0, one launch (start us, length us, event | category | flops | bytes accessed | tf_op | source)
XLA Modules:
  0.0 1437.8 jit_solution(2396205229600162140)
XLA Ops:
  13.5 51.0 %all-gather.9.cloned.1.call-done = bf16[4,256,1024]{2,1,0:T(8,128)(2,1)} async-done(((bf16[4,256,128]{2,1,0:T(8,128)(2,1)}), bf16[4,256,1024]{2,1,0:T(8,128)(2,1)}) %all-gather.9.cloned.1.call-update) | async-done | bytes 2097168 | tf_op jit(solution)/shard_map/all_gather | solution.py:214
  66.0 33.3 %all-gather.7.cloned.1.call-done = bf16[2048,1024]{1,0:T(8,128)(2,1)} async-done(((bf16[2048,256]{1,0:T(8,128)(2,1)}), bf16[2048,1024]{1,0:T(8,128)(2,1)}) %all-gather.7.cloned.1.call-update) | async-done | bytes 4194320 | tf_op jit(solution)/shard_map/all_gather | solution.py:26
  117.1 211.6 %while.64 = (s32[]{:T(128)}, bf16[4,2048,64]{1,2,0:T(8,128)(2,1)}, f32[4,2048]{1,0:T(4,128)}, bf16[4,2048,64]{2,1,0:T(8,128)(2,1)}, bf16[4,2048,64]{2,1,0:T(8,12...) while((s32[]{:T(128)}, bf16[4,2048,64]{1,2,0:T(8,128)(2,1)}, ...), condition=%wide.region_9.10_spmd.clone.clone, body=%wide.region_4.9_spmd.clone.sunk.clone | while | flops 283117568 | bytes 33639372 | solution.py:122
  120.1 47.3 %while.63 = (s32[]{:T(128)}, bf16[4,512,64]{1,2,0:T(8,128)(2,1)S(1)}, f32[4,512]{1,0:T(4,128)S(1)}, s32[4]{0:T(128)S(1)}, s32[2048]{0:T(1024)S(1)}, /*index=5*/s...) while((s32[]{:T(128)}, ...), condition=%wide.region_8.8_spmd, body=%wide.region_5.7_spmd.sunk | while | flops 283117568 | bytes 30460116 | solution.py:119
  173.0 47.3 %while.63 = (s32[]{:T(128)}, bf16[4,512,64]{1,2,0:T(8,128)(2,1)S(1)}, f32[4,512]{1,0:T(4,128)S(1)}, s32[4]{0:T(128)S(1)}, s32[2048]{0:T(1024)S(1)}, /*index=5*/s...) while((s32[]{:T(128)}, ...), condition=%wide.region_8.8_spmd, body=%wide.region_5.7_spmd.sunk | while | flops 283117568 | bytes 30460116 | solution.py:119
  225.9 47.3 %while.63 = (s32[]{:T(128)}, bf16[4,512,64]{1,2,0:T(8,128)(2,1)S(1)}, f32[4,512]{1,0:T(4,128)S(1)}, s32[4]{0:T(128)S(1)}, s32[2048]{0:T(1024)S(1)}, /*index=5*/s...) while((s32[]{:T(128)}, ...), condition=%wide.region_8.8_spmd, body=%wide.region_5.7_spmd.sunk | while | flops 283117568 | bytes 30460116 | solution.py:119
  278.8 47.3 %while.63 = (s32[]{:T(128)}, bf16[4,512,64]{1,2,0:T(8,128)(2,1)S(1)}, f32[4,512]{1,0:T(4,128)S(1)}, s32[4]{0:T(128)S(1)}, s32[2048]{0:T(1024)S(1)}, /*index=5*/s...) while((s32[]{:T(128)}, ...), condition=%wide.region_8.8_spmd, body=%wide.region_5.7_spmd.sunk | while | flops 283117568 | bytes 30460116 | solution.py:119
  337.9 69.4 %reduce-scatter.9.cloned.1.call-done = f32[2048,256]{1,0:T(8,128)} async-done(((f32[2048,1024]{1,0:T(8,128)}), f32[2048,256]{1,0:T(8,128)}) %reduce-scatter.9.cloned.1.call-update) | async-done | bytes 2097168 | tf_op jit(solution)/shard_map/reduce_scatter | solution.py:30
  425.7 84.2 %all-gather.13.cloned.1.call-done = bf16[3,1024,1024]{2,1,0:T(8,128)(2,1)} async-done(((bf16[3,1024,128]{2,1,0:T(8,128)(2,1)}), bf16[3,1024,1024]{2,1,0:T(8,128)(2,1)}) %all-gather.13.cloned.1.call-update) | async-done | bytes 6291472 | tf_op jit(solution)/shard_map/all_gather | solution.py:215
  509.9 35.3 %all-gather.11.cloned.1.call-done = bf16[2048,1024]{1,0:T(8,128)(2,1)} async-done(((bf16[2048,256]{1,0:T(8,128)(2,1)}), bf16[2048,1024]{1,0:T(8,128)(2,1)}) %all-gather.11.cloned.1.call-update) | async-done | bytes 4194320 | tf_op jit(solution)/shard_map/all_gather | solution.py:26
  575.7 71.8 %reduce-scatter.11.cloned.1.call-done = f32[2048,256]{1,0:T(8,128)} async-done(((f32[2048,1024]{1,0:T(8,128)}), f32[2048,256]{1,0:T(8,128)}) %reduce-scatter.11.cloned.1.call-update) | async-done | bytes 2097168 | tf_op jit(solution)/shard_map/reduce_scatter | solution.py:30
  689.3 35.5 %all-gather.15.cloned.1.call-done = bf16[2048,1024]{1,0:T(8,128)(2,1)} async-done(((bf16[2048,256]{1,0:T(8,128)(2,1)}), bf16[2048,1024]{1,0:T(8,128)(2,1)}) %all-gather.15.cloned.1.call-update) | async-done | bytes 4194320 | tf_op jit(solution)/shard_map/all_gather | solution.py:26
  724.8 20.5 %multiply_reduce_fusion.2 = (f32[1024]{0:T(1024)}, f32[1024]{0:T(1024)}, f32[2048,1024]{1,0:T(8,128)S(1)}, bf16[2048,1024]{1,0:T(8,128)(2,1)}) fusion(f32[2048,1024]{1,0:T(8,128)} %get-tuple-element.528, f32[2048,1024]{1,0:T(8,128)} %fusion.34, f32[1024]{0:T(1024)S(1)} %get-tuple-element.531, f32[1024]{0:T(1024)S(1)} %get-tuple-element.532, ...), kind=kOutput, calls=%fused_computation.61 | convolution fusion | flops 4341102592 | bytes 35672064 | tf_op jit(solution)/shard_map/td,fd->tf/dot_general | solution.py:278
  761.5 71.7 %reduce-scatter.13.cloned.1.call-done = f32[2048,256]{1,0:T(8,128)} async-done(((f32[2048,1024]{1,0:T(8,128)}), f32[2048,256]{1,0:T(8,128)}) %reduce-scatter.13.cloned.1.call-update) | async-done | bytes 2097168 | tf_op jit(solution)/shard_map/reduce_scatter | solution.py:30
  867.8 15.4 %fusion.31 = f32[2048,1024]{1,0:T(8,128)} fusion(bf16[2048,1024]{1,0:T(8,128)(2,1)} %all-gather.11.cloned.1.call-done, bf16[2048,1024]{1,0:T(8,128)(2,1)} %copy-done.21, bf16[2048,1024]{1,0:T(8,128)(2,1)} %get-tuple-element.507), kind=kOutput, calls=%fused_computation.70 | convolution fusion | flops 8608808960 | bytes 20971520 | tf_op jit(solution)/shard_map/tr,td->rd/dot_general | solution.py:292
  900.0 293.2 %while.66 = (s32[]{:T(128)}, f32[4,2048,64]{1,2,0:T(8,128)}, f32[4,2048,64]{1,2,0:T(8,128)}, bf16[4,2048,64]{1,2,0:T(8,128)(2,1)}, bf16[4,2048,64]{2,1,0:T(8,128...) while((s32[]{:T(128)}, f32[4,2048,64]{1,2,0:T(8,128)}, ...), condition=%wide.region_33.34_spmd.clone.clone, body=%wide.region_29.33_spmd.clone.sunk.clone | while | flops 687507456 | bytes 85191000 | solution.py:174
  905.3 64.5 %while.65 = (s32[]{:T(128)}, f32[2048,64]{0,1:T(8,128)}, f32[2048,64]{0,1:T(8,128)S(1)}, f32[4,512,64]{1,2,0:T(8,128)}, s32[4]{0:T(128)S(1)}, /*index=5*/s32[204...) while((s32[]{:T(128)}, f32[2048,64]{0,1:T(8,128)}, ...), condition=%wide.region_32.32_spmd.clone, body=%wide.region_30.31_spmd.clone.sunk | while | flops 687507456 | bytes 75736072 | solution.py:169
  978.5 64.5 %while.65 = (s32[]{:T(128)}, f32[2048,64]{0,1:T(8,128)}, f32[2048,64]{0,1:T(8,128)S(1)}, f32[4,512,64]{1,2,0:T(8,128)}, s32[4]{0:T(128)S(1)}, /*index=5*/s32[204...) while((s32[]{:T(128)}, f32[2048,64]{0,1:T(8,128)}, ...), condition=%wide.region_32.32_spmd.clone, body=%wide.region_30.31_spmd.clone.sunk | while | flops 687507456 | bytes 75736072 | solution.py:169
  1051.8 64.5 %while.65 = (s32[]{:T(128)}, f32[2048,64]{0,1:T(8,128)}, f32[2048,64]{0,1:T(8,128)S(1)}, f32[4,512,64]{1,2,0:T(8,128)}, s32[4]{0:T(128)S(1)}, /*index=5*/s32[204...) while((s32[]{:T(128)}, f32[2048,64]{0,1:T(8,128)}, ...), condition=%wide.region_32.32_spmd.clone, body=%wide.region_30.31_spmd.clone.sunk | while | flops 687507456 | bytes 75736072 | solution.py:169
  1125.1 64.5 %while.65 = (s32[]{:T(128)}, f32[2048,64]{0,1:T(8,128)}, f32[2048,64]{0,1:T(8,128)S(1)}, f32[4,512,64]{1,2,0:T(8,128)}, s32[4]{0:T(128)S(1)}, /*index=5*/s32[204...) while((s32[]{:T(128)}, f32[2048,64]{0,1:T(8,128)}, ...), condition=%wide.region_32.32_spmd.clone, body=%wide.region_30.31_spmd.clone.sunk | while | flops 687507456 | bytes 75736072 | solution.py:169
  1230.3 31.8 %reduce-scatter.19.cloned.1.call-done = f32[256,128]{1,0:T(8,128)} async-done(((f32[256,1024]{1,0:T(8,128)}), f32[256,128]{1,0:T(8,128)}) %reduce-scatter.19.cloned.1.call-update) | async-done | bytes 131088 | tf_op jit(solution)/shard_map/reduce_scatter | solution.py:352
  1262.1 77.8 %reduce-scatter.17.cloned.1.call-done = f32[768,128]{1,0:T(8,128)} async-done(((f32[768,1024]{1,0:T(8,128)}), f32[768,128]{1,0:T(8,128)}) %reduce-scatter.17.cloned.1.call-update) | async-done | bytes 393232 | tf_op jit(solution)/shard_map/reduce_scatter | solution.py:351
  1343.1 35.3 %all-reduce.1 = (f32[4,256]{1,0:T(4,128)S(1)}, f32[3,1024]{1,0:T(4,128)S(1)}, f32[3,256]{1,0:T(4,128)S(1)}, f32[2,1024]{1,0:T(2,128)S(1)}) all-reduce(f32[4,256]{1,0:T(4,128)S(1)} %get-tuple-element.489, f32[3,1024]{1,0:T(4,128)S(1)} %get-tuple-element.485, ...), channel_id=1, replica_groups=mesh['tok'=8,'dim'=4] {'tok'}, use_global_device_ids=true, to_apply=%region_40.41 | all-reduce | flops 6912 | bytes 55296 | tf_op jit(solution)/shard_map/psum | solution.py:377
  1383.6 37.1 %all-reduce = (f32[]{:T(128)}, f32[2]{0:T(128)S(1)}) all-reduce(f32[]{:T(128)S(6)} %add.258, f32[2]{0:T(128)S(1)} %broadcast_multiply_fusion.11), channel_id=1, replica_groups=mesh['tok'=8,'dim'=4] {'tok','dim'}, use_global_device_ids=true, to_apply=%region_56.57 | all-reduce | flops 3 | bytes 24 | tf_op jit(solution)/shard_map/psum | solution.py:392
  (995 shorter events, 682.2 us)
Async XLA Ops:
  7.2 57.3 %all-gather.9.cloned.1.call-start = ((), (), s32[]{:S(2)}) async-start(), calls=%async_computation.9 | async-start | bytes 2359296 | tf_op jit(solution)/shard_map/all_gather | solution.py:214
  9.1 90.2 %all-gather.7.cloned.1.call-start = ((), (), s32[]{:S(2)}) async-start(), calls=%async_computation.8 | async-start | bytes 5242880 | tf_op jit(solution)/shard_map/all_gather | solution.py:26
  9.8 397.5 %reduce-scatter.9.cloned.1.call-start = ((), (), s32[]{:S(2)}) async-start(), calls=%async_computation.10 | async-start | bytes 10485760 | tf_op jit(solution)/shard_map/reduce_scatter | solution.py:30
  335.4 79.7 %copy-start.40 = (f32[1,256]{1,0:T(1,128)S(1)}, f32[1,256]{1,0:T(1,128)}, u32[]{:S(2)}) copy-start(f32[1,256]{1,0:T(1,128)} %get-tuple-element.525) | copy-start | bytes 3076
  335.4 174.5 %all-gather.13.cloned.1.call-start = ((), (), s32[]{:S(2)}) async-start(), calls=%async_computation.12 | async-start | bytes 7077888 | tf_op jit(solution)/shard_map/all_gather | solution.py:215
  337.8 207.4 %all-gather.11.cloned.1.call-start = ((), (), s32[]{:S(2)}) async-start(), calls=%async_computation.11 | async-start | bytes 5242880 | tf_op jit(solution)/shard_map/all_gather | solution.py:26
  425.4 222.1 %reduce-scatter.11.cloned.1.call-start = ((), (), s32[]{:S(2)}) async-start(), calls=%async_computation.13 | async-start | bytes 10485760 | tf_op jit(solution)/shard_map/reduce_scatter | solution.py:30
  575.6 79.7 %copy-start.41 = (f32[1,256]{1,0:T(1,128)S(1)}, f32[1,256]{1,0:T(1,128)}, u32[]{:S(2)}) copy-start(f32[1,256]{1,0:T(1,128)} %get-tuple-element.526) | copy-start | bytes 3076
  575.6 149.1 %all-gather.15.cloned.1.call-start = ((), (), s32[]{:S(2)}) async-start(), calls=%async_computation.14 | async-start | bytes 5242880 | tf_op jit(solution)/shard_map/all_gather | solution.py:26
  689.2 143.9 %reduce-scatter.13.cloned.1.call-start = ((), (), s32[]{:S(2)}) async-start(), calls=%async_computation.15 | async-start | bytes 10485760 | tf_op jit(solution)/shard_map/reduce_scatter | solution.py:30
  761.2 131.7 %all-gather.17.cloned.1.call-start = ((), (), s32[]{:S(2)}) async-start(), calls=%async_computation.16 | async-start | bytes 5242880 | tf_op jit(solution)/shard_map/all_gather | solution.py:26
  856.3 365.9 %reduce-scatter.23.cloned.1.call-start = ((), (), s32[]{:S(2)}) async-start(), calls=%async_computation.21 | async-start | bytes 4718592 | tf_op jit(solution)/shard_map/reduce_scatter | solution.py:354
  866.5 355.8 %reduce-scatter.21.cloned.1.call-start = ((), (), s32[]{:S(2)}) async-start(), calls=%async_computation.20 | async-start | bytes 9437184 | tf_op jit(solution)/shard_map/reduce_scatter | solution.py:353
  883.2 378.9 %reduce-scatter.19.cloned.1.call-start = ((), (), s32[]{:S(2)}) async-start(), calls=%async_computation.19 | async-start | bytes 1179648 | tf_op jit(solution)/shard_map/reduce_scatter | solution.py:352
  1198.1 141.8 %reduce-scatter.17.cloned.1.call-start = ((), (), s32[]{:S(2)}) async-start(), calls=%async_computation.18 | async-start | bytes 3538944 | tf_op jit(solution)/shard_map/reduce_scatter | solution.py:351
  1212.8 213.6 %reduce-scatter.15.cloned.1.call-start = ((), (), s32[]{:S(2)}) async-start(), calls=%async_computation.17 | async-start | bytes 10485760 | tf_op jit(solution)/shard_map/reduce_scatter | solution.py:30
  1229.3 110.6 %copy-start.25 = (f32[4,256,128]{2,1,0:T(8,128)S(1)}, f32[4,256,128]{2,1,0:T(8,128)}, u32[]{:S(2)}) copy-start(f32[4,256,128]{2,1,0:T(8,128)} %param.28) | copy-start | bytes 1572868
  1229.3 110.6 %copy-start.36 = (f32[4,256,128]{2,1,0:T(8,128)S(1)}, f32[4,256,128]{2,1,0:T(8,128)}, u32[]{:S(2)}) copy-start(f32[4,256,128]{2,1,0:T(8,128)} %param.32) | copy-start | bytes 1572868
  1230.2 148.2 %copy-start.43 = (f32[3,256]{1,0:T(4,128)S(1)}, f32[3,256]{1,0:T(4,128)}, u32[]{:S(2)}) copy-start(f32[3,256]{1,0:T(4,128)} %param.30) | copy-start | bytes 9220
  1230.2 148.2 %copy-start.50 = (f32[3,256]{1,0:T(4,128)S(1)}, f32[3,256]{1,0:T(4,128)}, u32[]{:S(2)}) copy-start(f32[3,256]{1,0:T(4,128)} %param.36) | copy-start | bytes 9220
  1230.2 148.2 %copy-start.51 = (f32[3,256]{1,0:T(4,128)S(1)}, f32[3,256]{1,0:T(4,128)}, u32[]{:S(2)}) copy-start(f32[3,256]{1,0:T(4,128)} %param.37) | copy-start | bytes 9220
  1230.3 149.4 %copy-start.38 = (f32[2,1024]{1,0:T(2,128)S(1)}, f32[2,1024]{1,0:T(2,128)}, u32[]{:S(2)}) copy-start(f32[2,1024]{1,0:T(2,128)} %param.31) | copy-start | bytes 24580
  1230.3 149.4 %copy-start.46 = (f32[2,1024]{1,0:T(2,128)S(1)}, f32[2,1024]{1,0:T(2,128)}, u32[]{:S(2)}) copy-start(f32[2,1024]{1,0:T(2,128)} %param.38) | copy-start | bytes 24580
  1230.3 149.3 %copy-start.47 = (f32[2,1024]{1,0:T(2,128)S(1)}, f32[2,1024]{1,0:T(2,128)}, u32[]{:S(2)}) copy-start(f32[2,1024]{1,0:T(2,128)} %param.39) | copy-start | bytes 24580
  (223 other events, 887.8 us)
Sparse Core Ops, SparseCore 0:
  10.6 53.7 all-gather.8
  66.0 33.2 all-gather.6
  335.5 71.7 reduce-scatter.8
  410.0 99.9 all-gather.12
  512.0 33.2 all-gather.10
  575.7 71.6 reduce-scatter.10
  689.3 35.3 all-gather.14
  761.4 71.7 reduce-scatter.12
  856.5 36.4 all-gather.16
  896.9 88.4 reduce-scatter.22
  989.1 149.3 reduce-scatter.20
  1198.2 63.8 reduce-scatter.18
  1265.7 74.1 reduce-scatter.16
  1342.4 71.6 reduce-scatter.14
where the time goes:
time: 1450 us; the launch traced here: 1440 us
  waiting for transfers between devices  572 us (39%)
  matrix products  385 us (27%)
  local copies, waits for them, and re-layouts  164 us (11%)
  blocking collectives  121 us (8%)
  other arithmetic  109 us (8%)
  loops' own time  65.9 us (5%)
  between operations  19.5 us (1%)
    reduce_scatter x4, waiting for transfers between devices, own_rows(): lax.psum_scatter(partial_value, 'dim', scatter_dimension=1, tiled=True)  213 us
    all_gather x4, waiting for transfers between devices, whole_rows(): return lax.all_gather(shard, 'dim', axis=1, tiled=True)  113 us
    dot_general x32, matrix products, one_block(): jnp.einsum('qe,ke->qk', query_rows, key_head, preferred_element_type=jnp....  97.3 us
    all_gather x1, waiting for transfers between devices, local(): lax.all_gather(gated_weights.astype(jnp.bfloat16), 'tok', axis=2, tiled=T...  84.2 us
    reduce_scatter x1, waiting for transfers between devices, local(): lax.psum_scatter(delta_inward, 'tok', scatter_dimension=1, tiled=True)  77.8 us
    while x364, local copies, waits for them, and re-layouts  52.3 us
    all_gather x1, waiting for transfers between devices, local(): lax.all_gather(attention_weights.astype(jnp.bfloat16), 'tok', axis=2, til...  51 us
    dot_general x16, matrix products, one_block(): jnp.einsum('qk,ke->qe', probs_low, value_head, preferred_element_type=jnp...  50.5 us
  transfers between devices with their start and end apart: 14, of which 11 were waited for; matrix products, arithmetic and copies ran while one was open for 22% of the time, Pallas kernels for 0%

commit v1 on v0

v1 whole, which is shorter than its diff:
```python
import functools
import math

import jax
import jax.numpy as jnp
from jax import lax
from jax.experimental import pallas as pl
from jax.experimental.pallas import tpu as pltpu
from jax.sharding import PartitionSpec as P

D = 1024
HEAD = 64
FF = 4096
STEP = 4
BLK = 256

EPSILON = 1e-06
ADAM_EPSILON = 1e-08
BETA_ONE = 0.5
BETA_TWO = 0.5
LEARN_RATE = 1.5

F32 = jnp.float32
BF16 = jnp.bfloat16
SCALE_MODEL = D**-0.5
SCALE_HIDDEN = FF**-0.5
SCORE = HEAD**-0.5 * math.log2(math.e)
NEVER = 1 << 24


def dot_nt(left, right):
    return lax.dot_general(left, right, (((1,), (1,)), ((), ())), preferred_element_type=F32)


def dot_nn(left, right):
    return lax.dot_general(left, right, (((1,), (0,)), ((), ())), preferred_element_type=F32)


def split_low(values):
    high = values.astype(BF16)
    return high, (values - high.astype(F32)).astype(BF16)


def params():
    return pltpu.CompilerParams(vmem_limit_bytes=48 << 20)


def cost(flops, traffic, transcendentals=0):
    return pl.CostEstimate(
        flops=int(flops), bytes_accessed=int(traffic), transcendentals=int(transcendentals)
    )


def like(shape, dtype):
    return jax.ShapeDtypeStruct(shape, dtype)


def whole(*shape):
    return pl.BlockSpec(shape, lambda *_: (0,) * len(shape))


def rows(count, width):
    return pl.BlockSpec((count, width), lambda i, *_: (i, 0))


def head_matrix(width):
    row = lax.broadcasted_iota(jnp.int32, (width, width), 0)
    column = lax.broadcasted_iota(jnp.int32, (width, width), 1)
    return jnp.where(row // HEAD == column // HEAD, 1.0, 0.0).astype(BF16)


def head_mean(values, ones):
    high, low = split_low(values)
    return (dot_nn(high, ones) + dot_nn(low, ones)) * (1.0 / HEAD)


def project_kernel(
    pieces, me_ref, *refs
):
    piece_refs, (w_ref, gain_ref, all_ref, raw_ref, q_ref, k_ref, v_ref) = refs[:pieces], refs[pieces:]
    width = piece_refs[0].shape[1]
    for step, piece in enumerate(piece_refs):
        start = pl.multiple_of(jnp.bitwise_xor(me_ref[0], step) * width, width)
        all_ref[:, pl.ds(start, width)] = piece[...]
    projected = dot_nt(all_ref[...], w_ref[...]) * SCALE_MODEL
    raw_ref[...] = projected[:, : 2 * width]
    ones = head_matrix(width)
    for place, out in enumerate((q_ref, k_ref)):
        values = projected[:, place * width : (place + 1) * width]
        factor = lax.rsqrt(head_mean(values * values, ones) + EPSILON)
        out[...] = (values * factor * gain_ref[...]).astype(BF16)
    v_ref[...] = projected[:, 2 * width :].astype(BF16)


def project(me, pieces, weight, gain):
    count, width = pieces[0].shape
    depth = width * len(pieces)
    return pl.pallas_call(
        functools.partial(project_kernel, len(pieces)),
        grid_spec=pltpu.PrefetchScalarGridSpec(
            num_scalar_prefetch=1,
            grid=(count // BLK,),
            in_specs=[rows(BLK, width)] * len(pieces) + [whole(3 * width, depth), whole(1, width)],
            out_specs=[rows(BLK, depth), rows(BLK, 2 * width)] + [rows(BLK, width)] * 3,
        ),
        out_shape=[like((count, depth), BF16), like((count, 2 * width), F32)]
        + [like((count, width), BF16)] * 3,
        compiler_params=params(),
        cost_estimate=cost(6 * count * width * depth, count * (4 * depth + 14 * width)),
        name="project",
    )(me, *pieces, weight, gain)


def seq_start(place, starts):
    found = jnp.zeros_like(place)
    for start in starts:
        found = jnp.where(place >= start, start, found)
    return found


def later_starts(length_ref, count):
    starts, total = [], jnp.int32(0)
    for position in range(count - 1):
        total = total + length_ref[position]
        starts.append(total)
    return starts


def attend_kernel(count, length_ref, pad_ref, q_ref, k_ref, v_ref, o_ref, aux_ref, acc_ref):
    step = pl.program_id(0)
    first_row = step * BLK
    starts = later_starts(length_ref, count)
    first = seq_start(first_row, starts) // BLK
    lane = lax.broadcasted_iota(jnp.int32, (BLK, 128), 1)
    left = lane < HEAD
    heads = q_ref.shape[1] // HEAD
    zero = jnp.zeros((BLK, 128), BF16)
    one = jnp.ones((BLK, 128), BF16)
    sides = [left if head % 2 == 0 else ~left for head in range(heads)]
    columns = [slice(head // 2 * 128, (head // 2 + 1) * 128) for head in range(heads)]
    queries = [jnp.where(sides[h], q_ref[:, columns[h]], zero) for h in range(heads)]
    acc_ref[...] = jnp.zeros_like(acc_ref)
    row = first_row + lax.broadcasted_iota(jnp.int32, (BLK, 1), 0)
    row_start = seq_start(row, starts)

    def body(block, carry):
        key_rows = pl.ds(pl.multiple_of(block * BLK, BLK), BLK)
        key = block * BLK + lax.broadcasted_iota(jnp.int32, (1, BLK), 1)
        code = jnp.where(pad_ref[:, key_rows] == 1, key, NEVER)
        mask = ((code >= row_start) & (code <= row)) | (key == row)
        for h in range(heads):
            value = jnp.where(sides[h], v_ref[key_rows, columns[h]], one)
            scores = dot_nt(queries[h], k_ref[key_rows, columns[h]])
            powers = jnp.where(mask, jnp.exp2(scores * SCORE), 0.0).astype(BF16)
            acc_ref[h] += dot_nn(powers, value)
        return carry

    lax.fori_loop(first, step + 1, body, 0)
    for pair in range(heads // 2):
        even, odd = acc_ref[2 * pair], acc_ref[2 * pair + 1]
        total = jnp.where(left, odd, even)
        mixed = jnp.where(left, even, odd)
        o_ref[:, pair * 128 : (pair + 1) * 128] = (mixed / pltpu.roll(total, HEAD, 1)).astype(BF16)
        high, low = split_low(jnp.log2(total) * (-1.0 / SCORE))
        aux_ref[:, pair * 128 : (pair + 1) * 128] = jnp.where(
            lax.rem(lane, HEAD) < HEAD // 2, high, low
        )


def attend(lengths, pad_row, queries, keys, values):
    count, width = queries.shape
    heads = width // HEAD
    return pl.pallas_call(
        functools.partial(attend_kernel, lengths.shape[0]),
        grid_spec=pltpu.PrefetchScalarGridSpec(
            num_scalar_prefetch=1,
            grid=(count // BLK,),
            in_specs=[whole(1, count), rows(BLK, width), whole(count, width), whole(count, width)],
            out_specs=[rows(BLK, width)] * 2,
            scratch_shapes=[pltpu.VMEM((heads, BLK, 128), F32)],
        ),
        out_shape=[like((count, width), BF16)] * 2,
        compiler_params=params(),
        cost_estimate=cost(4 * count * count * width, 10 * count * width, count * count * heads // 3),
        name="attend",
    )(lengths, pad_row, queries, keys, values)


def attend_back_kernel(
    count, pieces, length_ref, me_ref, pad_ref, q_ref, aux_ref, k_ref, v_ref, o_ref, *refs
):
    piece_refs = refs[:pieces]
    dqt_ref, dk_ref, dv_ref, do_ref, inner_ref, key_acc, value_acc = refs[pieces:]
    step = pl.program_id(0)
    tokens, width = q_ref.shape
    heads = width // HEAD
    starts = later_starts(length_ref, count)
    lane = lax.broadcasted_iota(jnp.int32, (BLK, 128), 1)
    left = lane < HEAD
    zero = jnp.zeros((BLK, 128), BF16)
    one = jnp.ones((BLK, 128), BF16)
    sides = [left if head % 2 == 0 else ~left for head in range(heads)]
    columns = [slice(head // 2 * 128, (head // 2 + 1) * 128) for head in range(heads)]

    @pl.when(step == 0)
    def prepare():
        dqt_ref[...] = jnp.zeros_like(dqt_ref)
        part = tokens // pieces
        for place, piece in enumerate(piece_refs):
            start = pl.multiple_of(jnp.bitwise_xor(me_ref[0], place) * part, part)
            do_ref[pl.ds(start, part), :] = piece[...]
        row = lax.broadcasted_iota(jnp.int32, (128, 128), 0)
        column = lax.broadcasted_iota(jnp.int32, (128, 128), 1)
        other = jnp.where(row // HEAD != column // HEAD, 1.0, 0.0).astype(BF16)

        def inner(block, carry):
            here = pl.ds(pl.multiple_of(block * BLK, BLK), BLK)
            for pair in range(heads // 2):
                tile = slice(pair * 128, (pair + 1) * 128)
                high, low = split_low(do_ref[here, tile].astype(F32) * o_ref[here, tile].astype(F32))
                high, low = split_low(-(dot_nn(high, other) + dot_nn(low, other)))
                inner_ref[here, tile] = jnp.where(lax.rem(lane, HEAD) < HEAD // 2, high, low)
            return carry

        lax.fori_loop(0, tokens // BLK, inner, 0)

    key_rows = pl.ds(pl.multiple_of(step * BLK, BLK), BLK)
    last_key = step * BLK + BLK - 1
    end = jnp.int32(tokens)
    for start in reversed(starts):
        end = jnp.where(last_key < start, start, end)
    last = (end - 1) // BLK
    key_acc[...] = jnp.zeros_like(key_acc)
    value_acc[...] = jnp.zeros_like(value_acc)
    turned = jnp.transpose(k_ref[key_rows, :].astype(F32)).astype(BF16)
    keys, values = [], []
    for h in range(heads):
        hot = jnp.where((lax.rem(lane, HEAD // 2) == 0) & (~sides[h]), one, zero)
        for source, into in ((k_ref, keys), (v_ref, values)):
            tile = jnp.where(sides[h], source[key_rows, columns[h]], zero)
            into.append(jnp.concatenate([tile, hot], axis=1))
    key = step * BLK + lax.broadcasted_iota(jnp.int32, (BLK, 1), 0)
    code = jnp.where(pad_ref[key_rows, :] == 1, key, NEVER)

    def body(block, carry):
        here = pl.ds(pl.multiple_of(block * BLK, BLK), BLK)
        row = block * BLK + lax.broadcasted_iota(jnp.int32, (1, BLK), 1)
        mask = ((code >= seq_start(row, starts)) & (code <= row)) | (key == row)
        for h in range(heads):
            query, delta = q_ref[here, columns[h]], do_ref[here, columns[h]]
            scores = dot_nt(keys[h], jnp.concatenate([query, aux_ref[here, columns[h]]], axis=1))
            delta_probs = dot_nt(
                values[h], jnp.concatenate([delta, inner_ref[here, columns[h]]], axis=1)
            )
            probs = jnp.where(mask, jnp.exp2(scores * SCORE), 0.0)
            delta_scores = (probs * delta_probs).astype(BF16)
            value_acc[h] += dot_nn(probs.astype(BF16), delta)
            key_acc[h] += dot_nn(delta_scores, query)
            head_rows = slice(h * HEAD, (h + 1) * HEAD)
            dqt_ref[head_rows, here] += dot_nn(turned[head_rows, :], delta_scores)
        return carry

    lax.fori_loop(step, last + 1, body, 0)
    for pair in range(heads // 2):
        tile = slice(pair * 128, (pair + 1) * 128)
        dk_ref[:, tile] = jnp.where(left, key_acc[2 * pair], key_acc[2 * pair + 1])
        dv_ref[:, tile] = jnp.where(left, value_acc[2 * pair], value_acc[2 * pair + 1])


def attend_back(lengths, me, pad_column, queries, aux, keys, values, mixed, delta_pieces):
    count, width = queries.shape
    heads = width // HEAD
    pieces = len(delta_pieces)
    return pl.pallas_call(
        functools.partial(attend_back_kernel, lengths.shape[0], pieces),
        grid_spec=pltpu.PrefetchScalarGridSpec(
            num_scalar_prefetch=2,
            grid=(count // BLK,),
            in_specs=[whole(count, 1)]
            + [whole(count, width)] * 5
            + [whole(count // pieces, width)] * pieces,
            out_specs=[whole(width, count), rows(BLK, width), rows(BLK, width)],
            scratch_shapes=[
                pltpu.VMEM((count, width), BF16),
                pltpu.VMEM((count, width), BF16),
                pltpu.VMEM((heads, BLK, 128), F32),
                pltpu.VMEM((heads, BLK, 128), F32),
            ],
        ),
        out_shape=[like((width, count), F32), like((count, width), F32), like((count, width), F32)],
        compiler_params=params(),
        cost_estimate=cost(8 * count * count * width, 22 * count * width, count * count * heads // 3),
        name="attend_back",
    )(lengths, me, pad_column, queries, aux, keys, values, mixed, *delta_pieces)


def unit_of(values):
    factor = lax.rsqrt(jnp.mean(values * values, axis=1, keepdims=True) + EPSILON)
    return values * factor, factor


def unit_back(delta, unit, factor):
    return factor * (delta - unit * jnp.mean(delta * unit, axis=1, keepdims=True))


def mixer_kernel(pieces, *refs):
    mixed_refs, out_weights = refs[:pieces], refs[pieces : 2 * pieces]
    tokens_ref, alpha_ref, low_ref, one_ref, unit_ref, unit_factor, one_factor = refs[2 * pieces :]
    branch = dot_nn(mixed_refs[0][...], out_weights[0][...])
    for mixed, weight in zip(mixed_refs[1:], out_weights[1:]):
        branch += dot_nn(mixed[...], weight[...])
    unit, factor = unit_of(branch * SCALE_MODEL)
    unit_ref[...] = unit
    unit_factor[...] = jnp.broadcast_to(factor, unit_factor.shape)
    residual = tokens_ref[...].astype(F32)
    hidden, factor = unit_of(residual + alpha_ref[...] * (unit - residual))
    one_ref[...] = hidden
    one_factor[...] = jnp.broadcast_to(factor, one_factor.shape)
    low_ref[...] = hidden.astype(BF16)


def mixer(mixed_pieces, out_weights, me, tokens_all, alpha):
    count, width = mixed_pieces[0].shape
    pieces = len(mixed_pieces)
    depth = tokens_all.shape[1]
    blocks = count // BLK
    kernel = functools.partial(mixer_kernel, pieces)
    return pl.pallas_call(
        lambda me_ref, *refs: kernel(*refs),
        grid_spec=pltpu.PrefetchScalarGridSpec(
            num_scalar_prefetch=1,
            grid=(blocks,),
            in_specs=[rows(BLK, width)] * pieces
            + [whole(width, depth)] * pieces
            + [
                pl.BlockSpec((BLK, depth), lambda i, me_ref: (me_ref[0] * blocks + i, 0)),
                whole(1, depth),
            ],
            out_specs=[rows(BLK, depth)] * 3 + [rows(BLK, 128)] * 2,
        ),
        out_shape=[like((count, depth), BF16)]
        + [like((count, depth), F32)] * 2
        + [like((count, 128), F32)] * 2,
        compiler_params=params(),
        cost_estimate=cost(2 * count * depth * depth, 16 * count * depth + 2 * depth * depth),
        name="mixer",
    )(me, *mixed_pieces, *out_weights, tokens_all, alpha)


def turn_kernel(pieces, me_ref, *refs):
    own_ref, near_ref, far_ref, one_ref = refs[:4]
    seed_refs = refs[4 : 4 + pieces]
    pad_ref, alpha_ref = refs[4 + pieces : 6 + pieces]
    out_refs = refs[6 + pieces : 6 + 2 * pieces]
    low_ref, hidden_ref, alpha_sum, seed, layer = refs[6 + 2 * pieces :]
    width = seed_refs[0].shape[1]
    starts = [
        pl.multiple_of(jnp.bitwise_xor(me_ref[0], place) * width, width) for place in range(pieces)
    ]
    for start, piece in zip(starts, seed_refs):
        seed[:, pl.ds(start, width)] = piece[...]

    @pl.when(pl.program_id(0) == 0)
    def clear():
        alpha_sum[...] = jnp.zeros_like(alpha_sum)

    branch = (own_ref[...].astype(F32) + near_ref[...].astype(F32)) + far_ref[...].astype(F32)
    unit, unit_factor = unit_of(branch)
    hidden = one_ref[...]
    alpha = alpha_ref[...]
    layer_rows, layer_factor = unit_of(hidden + alpha * (unit - hidden))
    layer[...] = layer_rows.astype(BF16)
    for start, out in zip(starts, out_refs):
        out[...] = layer[:, pl.ds(start, width)]
    delta = unit_back(seed[...].astype(F32) * pad_ref[...], layer_rows, layer_factor)
    alpha_sum[...] += jnp.sum(delta * (unit - hidden), axis=0, keepdims=True)
    hidden_ref[...] = (1.0 - alpha) * delta
    low_ref[...] = unit_back(alpha * delta, unit, unit_factor).astype(BF16)


def turn(me, own, near, far, hidden_one, seed_pieces, pad_rows, alpha):
    count, depth = hidden_one.shape
    pieces = len(seed_pieces)
    width = depth // pieces
    return pl.pallas_call(
        functools.partial(turn_kernel, pieces),
        grid_spec=pltpu.PrefetchScalarGridSpec(
            num_scalar_prefetch=1,
            grid=(count // BLK,),
            in_specs=[rows(BLK, depth)] * 4
            + [rows(BLK, width)] * pieces
            + [rows(BLK, 1), whole(1, depth)],
            out_specs=[rows(BLK, width)] * pieces
            + [rows(BLK, depth), rows(BLK, depth), whole(1, depth)],
            scratch_shapes=[pltpu.VMEM((BLK, depth), BF16)] * 2,
        ),
        out_shape=[like((count, width), BF16)] * pieces
        + [like((count, depth), BF16), like((count, depth), F32), like((1, depth), F32)],
        compiler_params=params(),
        cost_estimate=cost(40 * count * depth, 20 * count * depth),
        name="turn",
    )(me, own, near, far, hidden_one, *seed_pieces, pad_rows, alpha)


def mixer_back_kernel(pieces, *refs):
    hidden_ref, own_ref, near_ref, far_ref, one_ref, unit_ref = refs[:6]
    one_factor, unit_factor, tokens_ref, alpha_ref = refs[6:10]
    out_weights = refs[10 : 10 + pieces]
    delta_refs = refs[10 + pieces : 10 + 2 * pieces]
    low_ref, direct_ref, alpha_sum = refs[10 + 2 * pieces :]

    @pl.when(pl.program_id(0) == 0)
    def clear():
        alpha_sum[...] = jnp.zeros_like(alpha_sum)

    delta = hidden_ref[...] + (
        (own_ref[...].astype(F32) + near_ref[...].astype(F32)) + far_ref[...].astype(F32)
    )
    unit = unit_ref[...]
    alpha = alpha_ref[...]
    delta = unit_back(delta, one_ref[...], one_factor[:, :1])
    alpha_sum[...] += jnp.sum(delta * (unit - tokens_ref[...].astype(F32)), axis=0, keepdims=True)
    direct_ref[...] = (1.0 - alpha) * delta
    low = unit_back(alpha * delta, unit, unit_factor[:, :1]).astype(BF16)
    low_ref[...] = low
    for weight, out in zip(out_weights, delta_refs):
        out[...] = (dot_nt(low, weight[...]) * SCALE_MODEL).astype(BF16)


def mixer_back(
    me, hidden, own, near, far, one, unit, one_factor, unit_factor, tokens_all, alpha, out_weights
):
    count, depth = one.shape
    pieces = len(out_weights)
    width = depth // pieces
    blocks = count // BLK
    kernel = functools.partial(mixer_back_kernel, pieces)
    return pl.pallas_call(
        lambda me_ref, *refs: kernel(*refs),
        grid_spec=pltpu.PrefetchScalarGridSpec(
            num_scalar_prefetch=1,
            grid=(blocks,),
            in_specs=[rows(BLK, depth)] * 6
            + [rows(BLK, 128)] * 2
            + [
                pl.BlockSpec((BLK, depth), lambda i, me_ref: (me_ref[0] * blocks + i, 0)),
                whole(1, depth),
            ]
            + [whole(width, depth)] * pieces,
            out_specs=[rows(BLK, width)] * pieces
            + [rows(BLK, depth), rows(BLK, depth), whole(1, depth)],
        ),
        out_shape=[like((count, width), BF16)] * pieces
        + [like((count, depth), BF16), like((count, depth), F32), like((1, depth), F32)],
        compiler_params=params(),
        cost_estimate=cost(2 * count * depth * depth, 28 * count * depth + 2 * depth * depth),
        name="mixer_back",
    )(me, hidden, own, near, far, one, unit, one_factor, unit_factor, tokens_all, alpha, *out_weights)


def gated_kernel(
    half, first_ref, second_ref, up_w, gate_w, down_w, gain_ref, all_ref, up_ref, gate_ref, mid_ref, out_ref
):
    step = pl.program_id(0)

    @pl.when(step < half)
    def from_first():
        all_ref[...] = first_ref[...]

    @pl.when(step >= half)
    def from_second():
        all_ref[...] = second_ref[...]

    hidden = all_ref[...]
    up = dot_nt(hidden, up_w[...]) * SCALE_MODEL
    gate = dot_nt(hidden, gate_w[...]) * SCALE_MODEL
    up_ref[...] = up.astype(BF16)
    gate_ref[...] = gate.astype(BF16)
    scaled = gain_ref[1:2, :] * gate
    middle = (gain_ref[0:1, :] * up * scaled * jax.nn.sigmoid(scaled)).astype(BF16)
    mid_ref[...] = middle
    out_ref[...] = (dot_nn(middle, down_w[...]) * SCALE_HIDDEN).astype(BF16)


def two_halves(block, half, depth):
    return [
        pl.BlockSpec((block, depth), lambda i: (jnp.minimum(i, half - 1), 0)),
        pl.BlockSpec((block, depth), lambda i: (jnp.maximum(i - half, 0), 0)),
    ]


def gated(first, second, up_w, gate_w, down_w, gains):
    count, depth = first.shape
    hidden = up_w.shape[0]
    half = count // BLK
    return pl.pallas_call(
        functools.partial(gated_kernel, half),
        grid=(2 * half,),
        in_specs=two_halves(BLK, half, depth) + [whole(hidden, depth)] * 3 + [whole(2, hidden)],
        out_specs=[rows(BLK, depth)] + [rows(BLK, hidden)] * 3 + [rows(BLK, depth)],
        out_shape=[like((2 * count, depth), BF16)]
        + [like((2 * count, hidden), BF16)] * 3
        + [like((2 * count, depth), BF16)],
        compiler_params=params(),
        cost_estimate=cost(
            12 * count * depth * hidden,
            12 * count * (depth + hidden) + 6 * depth * hidden,
            2 * count * hidden,
        ),
        name="gated",
    )(first, second, up_w, gate_w, down_w, gains)


def gated_back_kernel(
    half,
    first_ref,
    second_ref,
    up_ref,
    gate_ref,
    up_w,
    gate_w,
    down_w,
    gain_ref,
    all_ref,
    du_ref,
    dg_ref,
    out_ref,
    unit_ref,
):
    step = pl.program_id(0)

    @pl.when(step < half)
    def from_first():
        all_ref[...] = first_ref[...]

    @pl.when(step >= half)
    def from_second():
        all_ref[...] = second_ref[...]

    @pl.when(step == 0)
    def clear():
        unit_ref[...] = jnp.zeros_like(unit_ref)

    delta_middle = dot_nt(all_ref[...], down_w[...]) * SCALE_HIDDEN
    up = up_ref[...].astype(F32)
    gate = gate_ref[...].astype(F32)
    scaled = gain_ref[1:2, :] * gate
    sigmoid = jax.nn.sigmoid(scaled)
    shared = delta_middle * sigmoid
    delta_up = shared * scaled
    delta_gate = shared * (gain_ref[0:1, :] * up) * (1.0 + scaled * (1.0 - sigmoid))
    unit_ref[0:1, :] += jnp.sum(delta_up * up, axis=0, keepdims=True)
    unit_ref[1:2, :] += jnp.sum(delta_gate * gate, axis=0, keepdims=True)
    up_low = (gain_ref[0:1, :] * delta_up).astype(BF16)
    gate_low = (gain_ref[1:2, :] * delta_gate).astype(BF16)
    du_ref[...] = up_low
    dg_ref[...] = gate_low
    out_ref[...] = (
        (dot_nn(up_low, up_w[...]) + dot_nn(gate_low, gate_w[...])) * SCALE_MODEL
    ).astype(BF16)


def gated_back(first, second, up, gate, up_w, gate_w, down_w, gains):
    count, depth = first.shape
    hidden = up_w.shape[0]
    half = count // BLK
    return pl.pallas_call(
        functools.partial(gated_back_kernel, half),
        grid=(2 * half,),
        in_specs=two_halves(BLK, half, depth)
        + [rows(BLK, hidden)] * 2
        + [whole(hidden, depth)] * 3
        + [whole(2, hidden)],
        out_specs=[rows(BLK, depth)] + [rows(BLK, hidden)] * 2 + [rows(BLK, depth), whole(2, hidden)],
        out_shape=[like((2 * count, depth), BF16)]
        + [like((2 * count, hidden), BF16)] * 2
        + [like((2 * count, depth), BF16), like((2, hidden), F32)],
        compiler_params=params(),
        cost_estimate=cost(
            12 * count * depth * hidden,
            12 * count * (depth + hidden) + 6 * depth * hidden,
            2 * count * hidden,
        ),
        name="gated_back",
    )(first, second, up, gate, up_w, gate_w, down_w, gains)


def project_back_kernel(pieces, me_ref, dqt_ref, dk_ref, dv_ref, raw_ref, gain_ref, w_ref, direct_ref, *refs):
    low_ref, scale_sum, total = refs[0], refs[1 + pieces], refs[2 + pieces]
    part_refs = refs[1 : 1 + pieces]
    step = pl.program_id(0)
    width = dk_ref.shape[1]
    scale_head = HEAD**-0.5

    @pl.when(step == 0)
    def clear():
        scale_sum[...] = jnp.zeros_like(scale_sum)

    ones = head_matrix(width)
    gain = gain_ref[...]
    for place, delta in enumerate((jnp.transpose(dqt_ref[...]), dk_ref[...])):
        here = slice(place * width, (place + 1) * width)
        values = raw_ref[:, here]
        factor = lax.rsqrt(head_mean(values * values, ones) + EPSILON)
        unit = values * factor
        delta = delta * scale_head
        scale_sum[...] += jnp.sum(delta * unit, axis=0, keepdims=True)
        delta = gain * delta
        low_ref[:, here] = (factor * (delta - unit * head_mean(delta * unit, ones))).astype(BF16)
    low_ref[:, 2 * width :] = dv_ref[...].astype(BF16)
    total[...] = dot_nn(low_ref[...], w_ref[...]) * SCALE_MODEL
    own_blocks = direct_ref.shape[0] // BLK

    @pl.when(step // own_blocks == me_ref[0])
    def add_direct():
        start = pl.multiple_of(lax.rem(step, own_blocks) * BLK, BLK)
        total[...] += direct_ref[pl.ds(start, BLK), :]

    part = total.shape[1] // pieces
    for place, out in enumerate(part_refs):
        start = pl.multiple_of(jnp.bitwise_xor(me_ref[0], place) * part, part)
        out[...] = total[:, pl.ds(start, part)].astype(BF16)


def project_back(me, pieces, dqt, dk, dv, raw, gain, weight, direct):
    count, width = dk.shape
    depth = weight.shape[1]
    part = depth // pieces
    return pl.pallas_call(
        functools.partial(project_back_kernel, pieces),
        grid_spec=pltpu.PrefetchScalarGridSpec(
            num_scalar_prefetch=1,
            grid=(count // BLK,),
            in_specs=[
                pl.BlockSpec((width, BLK), lambda i, *_: (0, i)),
                rows(BLK, width),
                rows(BLK, width),
                rows(BLK, 2 * width),
                whole(1, width),
                whole(3 * width, depth),
                whole(*direct.shape),
            ],
            out_specs=[rows(BLK, 3 * width)] + [rows(BLK, part)] * pieces + [whole(1, width)],
            scratch_shapes=[pltpu.VMEM((BLK, depth), F32)],
        ),
        out_shape=[like((count, 3 * width), BF16)]
        + [like((count, part), BF16)] * pieces
        + [like((1, width), F32)],
        compiler_params=params(),
        cost_estimate=cost(6 * count * width * depth, count * (26 * width + 2 * depth)),
        name="project_back",
    )(me, dqt, dk, dv, raw, gain, weight, direct)


def trade(value, axis, offset):
    size = lax.axis_size(axis)
    return lax.ppermute(value, axis, [(i, i ^ offset) for i in range(size)])


def sum_over(value, axis):
    offset = 1
    while offset < lax.axis_size(axis):
        value = value + trade(value, axis, offset)
        offset *= 2
    return value


def gather_pieces(value):
    near = trade(value, "dim", 1)
    far = trade(value, "dim", 2)
    return [value, near, far, trade(far, "dim", 1)]


def scatter_sum(near, far):
    own, pair = near
    across, corner = far
    corner = trade(corner, "dim", 1)
    across = (across.astype(F32) + corner.astype(F32)).astype(BF16)
    return own, trade(pair, "dim", 1), trade(across, "dim", 2)


def grad_of(left_pieces, right_pieces, scale):
    total = None
    for left, right in zip(left_pieces, right_pieces):
        term = jnp.einsum("tr,td->rd", left, right, preferred_element_type=F32)
        total = term if total is None else total + term
    return (total * scale).astype(BF16)


def moment_update(weights, gradient, moment, square, fix_first, fix_second):
    moment_next = BETA_ONE * moment + (1.0 - BETA_ONE) * gradient
    square_next = BETA_TWO * square + (1.0 - BETA_TWO) * gradient * gradient
    stepped = weights - LEARN_RATE * (moment_next / fix_first) / (
        jnp.sqrt(square_next / fix_second) + ADAM_EPSILON
    )
    return (stepped, moment_next, square_next)


def local(
    inputs,
    cotangent,
    lengths,
    pad_mask,
    attention_weights,
    gated_weights,
    model_gains,
    unit_gains,
    attention_moment,
    attention_square,
    gated_moment,
    gated_square,
    model_moment,
    model_square,
    unit_moment,
    unit_square,
):
    token_count, width = inputs.shape
    parts = lax.axis_size("dim")
    hidden_here = gated_weights.shape[1]
    own_count = token_count // parts
    place = lax.axis_index("dim")
    me = place.astype(jnp.int32).reshape(1)
    length_row = lengths[0]

    def token_rows(value, offset):
        return lax.dynamic_slice_in_dim(value, (place ^ offset) * own_count, own_count, 0)

    def to_tokens(value):
        return [token_rows(value, 0)] + [
            trade(token_rows(value, r), "dim", r) for r in range(1, parts)
        ]

    token_pieces = gather_pieces(inputs)
    attention_low = lax.all_gather(attention_weights.astype(BF16), "tok", axis=2, tiled=True)
    weight_in = attention_low[:3].reshape(3 * width, D)
    out_weights = gather_pieces(attention_low[3])
    expand_low = lax.all_gather(gated_weights[:2].astype(BF16), "tok", axis=2, tiled=True)
    down_low = lax.all_gather(gated_weights[2].astype(BF16), "tok", axis=1, tiled=True)
    up_low, gate_low = expand_low[0], expand_low[1]
    alphas = sum_over(
        lax.dynamic_update_slice(jnp.zeros((2, D), F32), model_gains[1:], (0, place * width)), "dim"
    )
    alpha_mixer, alpha_gated = alphas[:1], alphas[1:]
    score_gain = model_gains[:1]

    tokens_all, raw, queries, keys, values = project(me, token_pieces, weight_in, score_gain)
    mixed, aux = attend(length_row, pad_mask[None, :], queries, keys, values)
    mixed_pieces = to_tokens(mixed)
    seed_pieces = to_tokens(cotangent)
    hidden_low, hidden_one, mixer_unit, mixer_factor, one_factor = mixer(
        mixed_pieces, out_weights, me, tokens_all, alpha_mixer
    )

    h_own, h_near, h_far, h_corner = gather_pieces(hidden_low)
    h_one, up_one, gate_one, mid_one, part_one = gated(
        h_own, h_near, up_low, gate_low, down_low, unit_gains
    )
    h_two, up_two, gate_two, mid_two, part_two = gated(
        h_far, h_corner, up_low, gate_low, down_low, unit_gains
    )
    own, near, far = scatter_sum(
        (part_one[:own_count], part_one[own_count:]), (part_two[:own_count], part_two[own_count:])
    )
    pad_rows = token_rows(pad_mask, 0).astype(F32)[:, None]
    *layer_pieces, delta_branch, delta_hidden, sum_gated = turn(
        me, own, near, far, hidden_one, seed_pieces, pad_rows, alpha_gated
    )
    layer_out = jnp.zeros((token_count, width), BF16)
    for r, piece in enumerate(layer_pieces):
        piece = piece if r == 0 else trade(piece, "dim", r)
        layer_out = lax.dynamic_update_slice(layer_out, piece, ((place ^ r) * own_count, 0))

    b_own, b_near, b_far, b_corner = gather_pieces(delta_branch)
    b_one, du_one, dg_one, back_one, unit_sum_one = gated_back(
        b_own, b_near, up_one, gate_one, up_low, gate_low, down_low, unit_gains
    )
    b_two, du_two, dg_two, back_two, unit_sum_two = gated_back(
        b_far, b_corner, up_two, gate_two, up_low, gate_low, down_low, unit_gains
    )
    own, near, far = scatter_sum(
        (back_one[:own_count], back_one[own_count:]), (back_two[:own_count], back_two[own_count:])
    )
    delta_down = grad_of((mid_one, mid_two), (b_one, b_two), SCALE_HIDDEN)
    delta_up = grad_of((du_one, du_two), (h_one, h_two), SCALE_MODEL)
    delta_gate = grad_of((dg_one, dg_two), (h_one, h_two), SCALE_MODEL)
    down_grad = lax.psum_scatter(delta_down, "tok", scatter_dimension=1, tiled=True)
    up_grad = lax.psum_scatter(delta_up, "tok", scatter_dimension=1, tiled=True)
    gate_grad = lax.psum_scatter(delta_gate, "tok", scatter_dimension=1, tiled=True)

    *delta_pieces, mixer_low, delta_direct, sum_mixer = mixer_back(
        me,
        delta_hidden,
        own,
        near,
        far,
        hidden_one,
        mixer_unit,
        one_factor,
        mixer_factor,
        tokens_all,
        alpha_mixer,
        out_weights,
    )
    delta_pieces = [delta_pieces[0]] + [
        trade(piece, "dim", r) for r, piece in enumerate(delta_pieces) if r
    ]
    delta_out = [grad_of((piece,), (mixer_low,), SCALE_MODEL) for piece in mixed_pieces]
    own, near, far = scatter_sum(delta_out[:2], delta_out[2:])
    delta_out = ((own.astype(F32) + near.astype(F32)) + far.astype(F32)).astype(BF16)
    dqt, dk, dv = attend_back(
        length_row, me, pad_mask[:, None], queries, aux, keys, values, mixed, delta_pieces
    )
    delta_project, *input_parts, scale_sum = project_back(
        me, parts, dqt, dk, dv, raw, score_gain, weight_in, delta_direct
    )
    delta_in = grad_of((delta_project,), (tokens_all,), SCALE_MODEL)
    own, near, far = scatter_sum(input_parts[:2], input_parts[2:])
    input_gradient = (own.astype(F32) + near.astype(F32)) + far.astype(F32)
    attention_grad = lax.psum_scatter(
        jnp.concatenate([delta_in, delta_out], axis=0), "tok", scatter_dimension=1, tiled=True
    )
    attention_grad = attention_grad.astype(F32).reshape(4, width, -1)
    gated_grad = jnp.stack([up_grad, gate_grad, down_grad]).astype(F32)

    alpha_sums = lax.dynamic_slice_in_dim(
        sum_over(jnp.concatenate([sum_mixer, sum_gated], axis=0), "dim"), place * width, width, 1
    )
    gains_sum = sum_over(
        jnp.concatenate(
            [scale_sum.reshape(-1), alpha_sums.reshape(-1), (unit_sum_one + unit_sum_two).reshape(-1)]
        ),
        "tok",
    )
    model_grad = gains_sum[: 3 * width].reshape(3, width)
    unit_grad = gains_sum[3 * width :].reshape(2, hidden_here)

    fix_first = 1.0 - BETA_ONE**STEP
    fix_second = 1.0 - BETA_TWO**STEP
    attention_stepped, moment_attention, square_attention = moment_update(
        attention_weights, attention_grad, attention_moment, attention_square, fix_first, fix_second
    )
    gated_stepped, moment_gated, square_gated = moment_update(
        gated_weights, gated_grad, gated_moment, gated_square, fix_first, fix_second
    )
    model_next, moment_model, square_model = moment_update(
        model_gains, model_grad, model_moment, model_square, fix_first, fix_second
    )
    unit_next, moment_unit, square_unit = moment_update(
        unit_gains, unit_grad, unit_moment, unit_square, fix_first, fix_second
    )
    token_groups = lax.axis_size("tok")
    local_square = (
        jnp.sum(attention_grad * attention_grad)
        + jnp.sum(gated_grad * gated_grad)
        + (jnp.sum(model_grad * model_grad) + jnp.sum(unit_grad * unit_grad)) / token_groups
    )
    row_sums = sum_over(
        jnp.concatenate(
            [
                jnp.sum(attention_stepped * attention_stepped, axis=2).reshape(-1),
                jnp.sum(gated_stepped * gated_stepped, axis=2).reshape(-1),
                local_square.reshape(1),
            ]
        ),
        "tok",
    )
    attention_rows = row_sums[: 4 * width].reshape(4, width, 1)
    gated_rows = row_sums[4 * width : -1].reshape(3, hidden_here, 1)
    attention_next = attention_stepped * lax.rsqrt(attention_rows / D + EPSILON)
    gated_next = gated_stepped * lax.rsqrt(gated_rows / D + EPSILON)
    totals = sum_over(jnp.concatenate([row_sums[-1:], jnp.sum(model_next[1:], axis=1)]), "dim")
    gradient_norm = jnp.sqrt(totals[:1])
    mean_alpha = totals[1:] / D
    return (
        layer_out,
        input_gradient,
        attention_next,
        attention_next.astype(BF16),
        moment_attention,
        square_attention,
        gated_next,
        gated_next.astype(BF16),
        moment_gated,
        square_gated,
        model_next,
        moment_model,
        square_model,
        unit_next,
        moment_unit,
        square_unit,
        gradient_norm,
        mean_alpha,
    )


def solution(mesh):
    tokens = P("tok", "dim")
    weights = P(None, "dim", "tok")
    gains = P(None, "dim")
    in_specs = (tokens, tokens, P("tok", None), P("tok"), weights, weights, gains, gains)
    in_specs += (weights,) * 4 + (gains,) * 4
    out_specs = (tokens, tokens) + (weights,) * 8 + (gains,) * 6 + (P(), P())
    return jax.shard_map(local, mesh=mesh, in_specs=in_specs, out_specs=out_specs, check_vma=False)
```

time: 1450 us -> 664 us (0.46)
  matrix products: 385 us -> 32.3 us
  waiting for transfers between devices: 572 us -> 337 us
  Pallas kernels: 0 us -> 144 us
  blocking collectives: 121 us -> 0 us
  local copies, waits for them, and re-layouts: 164 us -> 54 us
  other arithmetic: 109 us -> 30.9 us
  loops' own time: 65.9 us -> 0 us
  starting transfers between devices: 1.43 us -> 36.6 us
    dot_general x125 -> x11, matrix products: 385 us -> 32.3 us  [grad_of(): term = jnp.einsum('tr,td->rd', left, right, preferred_element_type=F32)]
    reduce_scatter x8 -> x0, waiting for transfers between devices: 323 us -> none  [the longest x4 213 us: own_rows(): lax.psum_scatter(partial_value, 'dim', scatter_dimension=1, tiled=True)]
    all_gather x6 -> x3, waiting for transfers between devices: 249 us -> 68.6 us  [the longest x1 43.8 us: local(): lax.all_gather(gated_weights[2].astype(BF16), 'tok', axis=1, tiled=True)]
    ppermute x0 -> x48, waiting for transfers between devices: none -> 174 us  [trade(): return lax.ppermute(value, axis, [(i, i ^ offset) for i in range(size)])]
    pallas_call x0 -> x11, Pallas kernels: none -> 144 us  [the longest x1 32.6 us: attend_back(): pl.pallas_call(functools.partial(attend_back_kernel, lengths.shape[0], pi...]
    psum x10 -> x0, blocking collectives: 121 us -> none  [the longest x8 48.4 us: token_sum(): return lax.psum(local_sum, 'dim')]
    unnamed x14 -> x11, waiting for transfers between devices: 0.91 us -> 94.8 us
    another operation x10 -> x0, loops' own time: 65.9 us -> none  [the longest x4 33.5 us: one_head(): lax.scan(one_block, (empty_acc, empty_acc), first_rows)]
  transfers between devices with their start and end apart: 14 -> 55, of which waited for: 11 -> 23; matrix products, arithmetic and copies ran while one was open for 22% -> 14% of each run, Pallas kernels for 0% -> 19%
where the time goes in v1:
time: 664 us; the launch traced here: 654 us
  waiting for transfers between devices  337 us (51%)
  Pallas kernels  144 us (22%)
  local copies, waits for them, and re-layouts  54 us (8%)
  starting transfers between devices  36.6 us (6%)
  matrix products  32.3 us (5%)
  other arithmetic  30.9 us (5%)
  between operations  19 us (3%)
    ppermute x48, waiting for transfers between devices, trade(): return lax.ppermute(value, axis, [(i, i ^ offset) for i in range(size)])  174 us
    unnamed x11, waiting for transfers between devices  94.8 us
    all_gather x1, waiting for transfers between devices, local(): lax.all_gather(gated_weights[2].astype(BF16), 'tok', axis=1, tiled=True)  43.8 us
    ppermute x48, starting transfers between devices, trade(): return lax.ppermute(value, axis, [(i, i ^ offset) for i in range(size)])  35.7 us
    unnamed x131, local copies, waits for them, and re-layouts  32.6 us
    pallas_call x1, Pallas kernels, attend_back(): pl.pallas_call(functools.partial(attend_back_kernel, lengths.shape[0], pi...  32.6 us
    dot_general x11, matrix products, grad_of(): term = jnp.einsum('tr,td->rd', left, right, preferred_element_type=F32)  32.3 us
    pallas_call x2, Pallas kernels, gated_back(): pl.pallas_call(functools.partial(gated_back_kernel, half), grid=(2 * half...  29 us
  transfers between devices with their start and end apart: 55, of which 23 were waited for; matrix products, arithmetic and copies ran while one was open for 14% of the time, Pallas kernels for 19%

profile of v1, /device:TPU:0, one launch (start us, length us, event | category | flops | bytes accessed | tf_op | source)
XLA Modules:
  0.0 653.6 jit_solution(13187166367287287989)
XLA Ops:
  14.6 23.3 %collective-permute-done.1.refs_2_ = bf16[2048,256]{1,0:T(8,128)(2,1)} collective-permute-done((bf16[2048,256]{1,0:T(8,128)(2,1)S(1)}, bf16[2048,256]{1,0:T(8,128)(2,1)}, u32[]{:S(2)}, u32[]{:S(2)}) %collective-permute-start.1) | collective-permute-done | bytes 1048608 | tf_op jit(solution)/shard_map/ppermute | solution.py:657
  39.3 24.8 %all-gather.5.cloned.1.call-done = bf16[4,256,1024]{2,1,0:T(8,128)(2,1)} async-done(((bf16[4,256,128]{2,1,0:T(8,128)(2,1)}), bf16[4,256,1024]{2,1,0:T(8,128)(2,1)}) %all-gather.5.cloned.1.call-update) | async-done | bytes 2097168 | tf_op jit(solution)/shard_map/all_gather | solution.py:734
  70.1 10.1 %project.1 = (bf16[2048,1024]{1,0:T(8,128)(2,1)}, f32[2048,512]{1,0:T(8,128)}, bf16[2048,256]{1,0:T(8,128)(2,1)S(1)}, bf16[2048,256]{1,0:T(8,128)(2,1)S(1)}, bf16[2048,256]{1,0:T(8,128)(2,1)S(1)}) custom-call(s32[1]{0:T(128)} %bitcast.me_ref, bf16[2048,256]{1,0:T(8,128)(2,1)S(1)} %copy-done.19, bf16[2048,256]{1,0:T(8,128)(2,1)} %collective-permute-done.refs_1_, ...), custom_call_target="tpu_custom_call" | custom-call | flops 3221225472 | bytes 15728640 | tf_op jit(solution)/shard_map/project/pallas_call | solution.py:98
  80.8 16.2 %attend.1 = (bf16[2048,256]{1,0:T(8,128)(2,1)S(1)}, bf16[2048,256]{1,0:T(8,128)(2,1)S(1)}) custom-call(s32[3]{0:T(128)S(1)} %bitcast.67, s32[1,2048]{1,0:T(1,128)S(1)} %bitcast.63, bf16[2048,256]{1,0:T(8,128)(2,1)S(1)} %get-tuple-element.73.q_ref, bf16[2048,256]{1,0:T(8,128)(2,1)S(1)} %get-tuple-element.74.k_ref, bf16[2048,256]{1,0:T(8,128)(2,1)S(1)} %get-tuple-element.75.v_ref), custom_call_target="tpu_custom_call" | custom-call | flops 4294967296 | bytes 5242880 | tf_op jit(solution)/shard_map/attend/pallas_call | solution.py:173
  99.2 7.3 %collective-permute-done.4.refs_2_ = bf16[512,256]{1,0:T(8,128)(2,1)S(1)} collective-permute-done((bf16[512,256]{1,0:T(8,128)(2,1)S(1)}, bf16[512,256]{1,0:T(8,128)(2,1)S(1)}, u32[]{:S(2)}, u32[]{:S(2)}) %collective-permute-start.4) | collective-permute-done | bytes 262176 | tf_op jit(solution)/shard_map/ppermute | solution.py:657
  118.3 24.6 %collective-permute-done.13.first_ref = bf16[512,1024]{1,0:T(8,128)(2,1)} collective-permute-done((bf16[512,1024]{1,0:T(8,128)(2,1)}, bf16[512,1024]{1,0:T(8,128)(2,1)}, u32[]{:S(2)}, u32[]{:S(2)}) %collective-permute-start.13) | collective-permute-done | bytes 1048608 | tf_op jit(solution)/shard_map/ppermute | solution.py:657
  148.1 43.8 %all-gather.9.cloned.1.call-done = bf16[1,1024,1024]{2,1,0:T(8,128)(2,1)} async-done(((bf16[1,1024,128]{2,1,0:T(8,128)(2,1)}), bf16[1,1024,1024]{2,1,0:T(8,128)(2,1)}) %all-gather.9.cloned.1.call-update) | async-done | bytes 2097168 | tf_op jit(solution)/shard_map/all_gather | solution.py:738
  191.9 12.7 %gated.3 = (bf16[1024,1024]{1,0:T(8,128)(2,1)S(1)}, bf16[1024,1024]{1,0:T(8,128)(2,1)}, bf16[1024,1024]{1,0:T(8,128)(2,1)}, bf16[1024,1024]{1,0:T(8,128)(2,1)}, bf16[1024,1024]{1,0:T(8,128)(2,1)}) custom-call(bf16[512,1024]{1,0:T(8,128)(2,1)} %collective-permute-done.13.first_ref, bf16[512,1024]{1,0:T(8,128)(2,1)} %collective-permute-done.14.second_ref, ...), custom_call_target="tpu_custom_call" | custom-call | flops 6442450944 | bytes 18874368 | tf_op jit(solution)/shard_map/gated/pallas_call | solution.py:496
  207.3 12.7 %gated.2 = (bf16[1024,1024]{1,0:T(8,128)(2,1)S(1)}, bf16[1024,1024]{1,0:T(8,128)(2,1)}, bf16[1024,1024]{1,0:T(8,128)(2,1)}, bf16[1024,1024]{1,0:T(8,128)(2,1)}, bf16[1024,1024]{1,0:T(8,128)(2,1)}) custom-call(bf16[512,1024]{1,0:T(8,128)(2,1)} %get-tuple-element.78.first_ref, bf16[512,1024]{1,0:T(8,128)(2,1)} %collective-permute-done.11.second_ref, ...), custom_call_target="tpu_custom_call" | custom-call | flops 6442450944 | bytes 18874368 | tf_op jit(solution)/shard_map/gated/pallas_call | solution.py:496
  230.7 26.7 %collective-permute-done.18.refs_6_ = bf16[512,256]{1,0:T(8,128)(2,1)} collective-permute-done((bf16[512,256]{1,0:T(8,128)(2,1)}, bf16[512,256]{1,0:T(8,128)(2,1)}, u32[]{:S(2)}, u32[]{:S(2)}) %collective-permute-start.18) | collective-permute-done | bytes 262176 | tf_op jit(solution)/shard_map/ppermute | solution.py:657
  273.1 23.9 %collective-permute-done.25.first_ref = bf16[512,1024]{1,0:T(8,128)(2,1)S(1)} collective-permute-done((bf16[512,1024]{1,0:T(8,128)(2,1)S(1)}, bf16[512,1024]{1,0:T(8,128)(2,1)S(1)}, u32[]{:S(2)}, u32[]{:S(2)}) %collective-permute-start.25) | collective-permute-done | bytes 1048608 | tf_op jit(solution)/shard_map/ppermute | solution.py:657
  297.0 14.6 %gated_back.2 = (bf16[1024,1024]{1,0:T(8,128)(2,1)S(1)}, bf16[1024,1024]{1,0:T(8,128)(2,1)}, bf16[1024,1024]{1,0:T(8,128)(2,1)}, bf16[1024,1024]{1,0:T(8,128)(2,1)}, f32[2,1024]{1,0:T(2,128)S(1)}) custom-call(bf16[512,1024]{1,0:T(8,128)(2,1)S(1)} %get-tuple-element.88.first_ref, bf16[512,1024]{1,0:T(8,128)(2,1)S(1)} %collective-permute-done.23.second_ref, ...), custom_call_target="tpu_custom_call" | custom-call | flops 6442450944 | bytes 18874368 | tf_op jit(solution)/shard_map/gated_back/pallas_call | solution.py:567
  316.4 14.4 %gated_back.3 = (bf16[1024,1024]{1,0:T(8,128)(2,1)S(1)}, bf16[1024,1024]{1,0:T(8,128)(2,1)}, bf16[1024,1024]{1,0:T(8,128)(2,1)}, bf16[1024,1024]{1,0:T(8,128)(2,1)}, f32[2,1024]{1,0:T(2,128)S(1)}) custom-call(bf16[512,1024]{1,0:T(8,128)(2,1)S(1)} %collective-permute-done.25.first_ref, bf16[512,1024]{1,0:T(8,128)(2,1)S(1)} %collective-permute-done.26.second_ref, ...), custom_call_target="tpu_custom_call" | custom-call | flops 6442450944 | bytes 18874368 | tf_op jit(solution)/shard_map/gated_back/pallas_call | solution.py:567
  332.1 5.6 multiply_convert_fusion.2
  374.0 15.1 %collective-permute-done.28.refs_3_ = bf16[512,1024]{1,0:T(8,128)(2,1)} collective-permute-done((bf16[512,1024]{1,0:T(8,128)(2,1)}, bf16[512,1024]{1,0:T(8,128)(2,1)}, u32[]{:S(2)}, u32[]{:S(2)}) %collective-permute-start.28) | collective-permute-done | bytes 1048608 | tf_op jit(solution)/shard_map/ppermute | solution.py:657
  391.0 6.7 %mixer_back.1 = (bf16[512,256]{1,0:T(8,128)(2,1)S(1)}, bf16[512,256]{1,0:T(8,128)(2,1)S(1)}, bf16[512,256]{1,0:T(8,128)(2,1)S(1)}, bf16[512,256]{1,0:T(8,128)(2,...) custom-call(s32[1]{0:T(128)} %bitcast.me_ref, ...), custom_call_target="tpu_custom_call" | custom-call | flops 1073741824 | bytes 16777216 | tf_op jit(solution)/shard_map/mixer_back/pallas_call | solution.py:438
  401.2 5.7 collective-permute-done.30.refs_2_
  411.7 32.6 %attend_back.1 = (f32[256,2048]{1,0:T(8,128)}, f32[2048,256]{1,0:T(8,128)}, f32[2048,256]{1,0:T(8,128)}) custom-call(s32[3]{0:T(128)S(1)} %bitcast.68, s32[1]{0:T(128)} %bitcast.me_ref, s32[2048,1]{1,0:T(8,128)S(1)} %copy-done.4, bf16[2048,256]{1,0:T(8,128)(2,1)S(1)} %copy-done.37, bf16[2048,256]{1,0:T(8,128)(2,1)S(1)} %copy-done.42, ...), custom_call_target="tpu_custom_call" | custom-call | flops 8589934592 | bytes 11534336 | tf_op jit(solution)/shard_map/attend_back/pallas_call | solution.py:274
  444.3 13.4 %project_back.1 = (bf16[2048,768]{1,0:T(8,128)(2,1)}, bf16[2048,256]{1,0:T(8,128)(2,1)S(1)}, bf16[2048,256]{1,0:T(8,128)(2,1)S(1)}, bf16[2048,256]{1,0:T(8,128)(...) custom-call(s32[1]{0:T(128)} %bitcast.me_ref, f32[256,2048]{1,0:T(8,128)} %get-tuple-element.102.dqt_ref, ...), custom_call_target="tpu_custom_call" | custom-call | flops 3221225472 | bytes 17825792 | tf_op jit(solution)/shard_map/project_back/pallas_call | solution.py:629
  465.1 7.2 %collective-permute-done.37 = bf16[256,1024]{1,0:T(8,128)(2,1)S(1)} collective-permute-done((bf16[256,1024]{1,0:T(8,128)(2,1)S(1)}, bf16[256,1024]{1,0:T(8,128)(2,1)S(1)}, u32[]{:S(2)}, u32[]{:S(2)}) %collective-permute-start.37) | collective-permute-done | bytes 524320 | tf_op jit(solution)/shard_map/ppermute | solution.py:657
  483.3 10.1 %collective-permute-done.39 = f32[2,1024]{1,0:T(2,128)S(1)} collective-permute-done((f32[2,1024]{1,0:T(2,128)S(1)}, f32[2,1024]{1,0:T(2,128)S(1)}, u32[]{:S(2)}, u32[]{:S(2)}) %collective-permute-start.39) | collective-permute-done | bytes 8224 | tf_op jit(solution)/shard_map/ppermute | solution.py:657
  515.9 32.2 %reduce-scatter.19.cloned.1.call-done = bf16[128,1024]{1,0:T(8,128)(2,1)} async-done(((bf16[1024,1024]{1,0:T(8,128)(2,1)}), bf16[128,1024]{1,0:T(8,128)(2,1)}) %reduce-scatter.19.cloned.1.call-update) | async-done | bytes 262160
  549.2 6.5 multiply_reduce_fusion
  555.6 62.5 %reduce-scatter.13.cloned.1.call-done = bf16[128,1024]{1,0:T(8,128)(2,1)} async-done(((bf16[1024,1024]{1,0:T(8,128)(2,1)}), bf16[128,1024]{1,0:T(8,128)(2,1)}) %reduce-scatter.13.cloned.1.call-update) | async-done | bytes 262160
  (312 shorter events, 182.2 us)
Async XLA Ops:
  7.2 56.9 %all-gather.5.cloned.1.call-start = ((), (), s32[]{:S(2)}) async-start(), calls=%async_computation.4 | async-start | bytes 2359296 | tf_op jit(solution)/shard_map/all_gather | solution.py:734
  9.0 134.4 %all-gather.7.cloned.1.call-start = ((), (), s32[]{:S(2)}) async-start(), calls=%async_computation.5 | async-start | bytes 4718592 | tf_op jit(solution)/shard_map/all_gather | solution.py:737
  11.5 180.4 %all-gather.9.cloned.1.call-start = ((), (), s32[]{:S(2)}) async-start(), calls=%async_computation.6 | async-start | bytes 2359296 | tf_op jit(solution)/shard_map/all_gather | solution.py:738
  11.6 26.3 %collective-permute-start.1 = (bf16[2048,256]{1,0:T(8,128)(2,1)S(1)}, bf16[2048,256]{1,0:T(8,128)(2,1)}, u32[]{:S(2)}, u32[]{:S(2)}) collective-permute-start(bf16[2048,256]{1,0:T(8,128)(2,1)S(1)} %copy-done.19), channel_id=1, source_target_pairs={{0,2},{1,3},{2,0},{3,1},{4,6},{5,7},{6,4},{7,5},{8,10},{9,11},{10,... | collective-permute-start | bytes 3145736 | tf_op jit(solution)/shard_map/ppermute | solution.py:657
  14.6 55.4 %collective-permute-start = (bf16[2048,256]{1,0:T(8,128)(2,1)S(1)}, bf16[2048,256]{1,0:T(8,128)(2,1)}, u32[]{:S(2)}, u32[]{:S(2)}) collective-permute-start(bf16[2048,256]{1,0:T(8,128)(2,1)S(1)} %copy-done.19), channel_id=1, source_target_pairs={{0,1},{1,0},{2,3},{3,2},{4,5},{5,4},{6,7},{7,6},{8,9},{9,8},{10,11... | collective-permute-start | bytes 3145736 | tf_op jit(solution)/shard_map/ppermute | solution.py:657
  37.9 32.2 %collective-permute-start.2 = (bf16[2048,256]{1,0:T(8,128)(2,1)}, bf16[2048,256]{1,0:T(8,128)(2,1)}, u32[]{:S(2)}, u32[]{:S(2)}) collective-permute-start(bf16[2048,256]{1,0:T(8,128)(2,1)} %collective-permute-done.1.refs_2_), channel_id=1, source_target_pairs={{0,1},{1,0},{2,3},{3,2},{4,5},{5,4},{6,7},{7,6},{8,9},{9,8},{10,11... | collective-permute-start | bytes 3145736 | tf_op jit(solution)/shard_map/ppermute | solution.py:657
  37.9 28.8 %collective-permute-start.9 = (f32[2,1024]{1,0:T(2,128)S(1)}, f32[2,1024]{1,0:T(2,128)S(1)}, u32[]{:S(2)}, u32[]{:S(2)}) collective-permute-start(f32[2,1024]{1,0:T(2,128)S(1)} %constant_dynamic-update-slice_fusion.5), channel_id=1, source_target_pairs={{0,1},{1,0},{2,3},{3,2},{4,5},{5,4},{6,7},{7,6},{8,9},{9,8},{10,11... | collective-permute-start | bytes 24584 | tf_op jit(solution)/shard_map/ppermute | solution.py:657
  39.2 474.3 %reduce-scatter.15.cloned.1.call-start = ((), (), s32[]{:S(2)}) async-start(), calls=%async_computation.8 | async-start | bytes 2359296
  66.8 32.0 %collective-permute-start.10 = (f32[2,1024]{1,0:T(2,128)S(1)}, f32[2,1024]{1,0:T(2,128)S(1)}, u32[]{:S(2)}, u32[]{:S(2)}) collective-permute-start(f32[2,1024]{1,0:T(2,128)S(1)} %constant_dynamic-update-slice_fusion.4), channel_id=1, source_target_pairs={{0,2},{1,3},{2,0},{3,1},{4,6},{5,7},{6,4},{7,5},{8,10},{9,11},{10,... | collective-permute-start | bytes 24584 | tf_op jit(solution)/shard_map/ppermute | solution.py:657
  67.4 43.8 %collective-permute-start.6 = (bf16[256,1024]{1,0:T(8,128)(2,1)S(1)}, bf16[256,1024]{1,0:T(8,128)(2,1)S(1)}, u32[]{:S(2)}, u32[]{:S(2)}) collective-permute-start(bf16[256,1024]{1,0:T(8,128)(2,1)S(1)} %slice_bitcast_fusion.2.refs_4_.refs_10_), channel_id=1, source_target_pairs={{0,1},{1,0},{2,3},{3,2},{4,5},{5,4},{6,7},{7,6},{8,9},{9,8},{10,11... | collective-permute-start | bytes 1572872 | tf_op jit(solution)/shard_map/ppermute | solution.py:657
  80.2 30.9 %collective-permute-start.8 = (bf16[256,1024]{1,0:T(8,128)(2,1)S(1)}, bf16[256,1024]{1,0:T(8,128)(2,1)S(1)}, u32[]{:S(2)}, u32[]{:S(2)}) collective-permute-start(bf16[256,1024]{1,0:T(8,128)(2,1)S(1)} %collective-permute-done.7.refs_6_.refs_12_), channel_id=1, source_target_pairs={{0,1},{1,0},{2,3},{3,2},{4,5},{5,4},{6,7},{7,6},{8,9},{9,8},{10,11... | collective-permute-start | bytes 1572872 | tf_op jit(solution)/shard_map/ppermute | solution.py:657
  142.9 49.0 %collective-permute-start.14 = (bf16[512,1024]{1,0:T(8,128)(2,1)}, bf16[512,1024]{1,0:T(8,128)(2,1)}, u32[]{:S(2)}, u32[]{:S(2)}) collective-permute-start(bf16[512,1024]{1,0:T(8,128)(2,1)} %collective-permute-done.13.first_ref), channel_id=1, source_target_pairs={{0,1},{1,0},{2,3},{3,2},{4,5},{5,4},{6,7},{7,6},{8,9},{9,8},{10,11... | collective-permute-start | bytes 3145736 | tf_op jit(solution)/shard_map/ppermute | solution.py:657
  142.9 64.5 %collective-permute-start.11 = (bf16[512,1024]{1,0:T(8,128)(2,1)}, bf16[512,1024]{1,0:T(8,128)(2,1)}, u32[]{:S(2)}, u32[]{:S(2)}) collective-permute-start(bf16[512,1024]{1,0:T(8,128)(2,1)} %get-tuple-element.78.first_ref), channel_id=1, source_target_pairs={{0,1},{1,0},{2,3},{3,2},{4,5},{5,4},{6,7},{7,6},{8,9},{9,8},{10,11... | collective-permute-start | bytes 3145736 | tf_op jit(solution)/shard_map/ppermute | solution.py:657
  223.5 37.6 %collective-permute-start.12 = (bf16[512,1024]{1,0:T(8,128)(2,1)}, bf16[512,1024]{1,0:T(8,128)(2,1)}, u32[]{:S(2)}, u32[]{:S(2)}) collective-permute-start(bf16[512,1024]{1,0:T(8,128)(2,1)} %get-tuple-element.150), channel_id=1, source_target_pairs={{0,1},{1,0},{2,3},{3,2},{4,5},{5,4},{6,7},{7,6},{8,9},{9,8},{10,11... | collective-permute-start | bytes 3145736 | tf_op jit(solution)/shard_map/ppermute | solution.py:657
  225.4 35.7 %collective-permute-start.16 = (bf16[512,1024]{1,0:T(8,128)(2,1)}, bf16[512,1024]{1,0:T(8,128)(2,1)}, u32[]{:S(2)}, u32[]{:S(2)}) collective-permute-start(bf16[512,1024]{1,0:T(8,128)(2,1)} %add_convert_fusion.2), channel_id=1, source_target_pairs={{0,2},{1,3},{2,0},{3,1},{4,6},{5,7},{6,4},{7,5},{8,10},{9,11},{10,... | collective-permute-start | bytes 3145736 | tf_op jit(solution)/shard_map/ppermute | solution.py:657
  227.9 29.5 %collective-permute-start.18 = (bf16[512,256]{1,0:T(8,128)(2,1)}, bf16[512,256]{1,0:T(8,128)(2,1)}, u32[]{:S(2)}, u32[]{:S(2)}) collective-permute-start(bf16[512,256]{1,0:T(8,128)(2,1)} %get-tuple-element.155), channel_id=1, source_target_pairs={{0,2},{1,3},{2,0},{3,1},{4,6},{5,7},{6,4},{7,5},{8,10},{9,11},{10,... | collective-permute-start | bytes 786440 | tf_op jit(solution)/shard_map/ppermute | solution.py:657
  228.4 32.7 %collective-permute-start.19 = (bf16[512,256]{1,0:T(8,128)(2,1)}, bf16[512,256]{1,0:T(8,128)(2,1)}, u32[]{:S(2)}, u32[]{:S(2)}) collective-permute-start(bf16[512,256]{1,0:T(8,128)(2,1)} %get-tuple-element.152), channel_id=1, source_target_pairs={{0,3},{1,2},{2,1},{3,0},{4,7},{5,6},{6,5},{7,4},{8,11},{9,10},{10,... | collective-permute-start | bytes 786440 | tf_op jit(solution)/shard_map/ppermute | solution.py:657
  341.7 173.1 %reduce-scatter.17.cloned.1.call-start = ((), (), s32[]{:S(2)}) async-start(), calls=%async_computation.9 | async-start | bytes 2359296
  354.7 193.4 %reduce-scatter.19.cloned.1.call-start = ((), (), s32[]{:S(2)}) async-start(), calls=%async_computation.10 | async-start | bytes 2359296
  372.4 245.8 %reduce-scatter.13.cloned.1.call-start = ((), (), s32[]{:S(2)}) async-start(), calls=%async_computation.7 | async-start | bytes 2359296
  400.1 57.6 %collective-permute-start.36 = (bf16[256,1024]{1,0:T(8,128)(2,1)S(1)}, bf16[256,1024]{1,0:T(8,128)(2,1)S(1)}, u32[]{:S(2)}, u32[]{:S(2)}) collective-permute-start(bf16[256,1024]{1,0:T(8,128)(2,1)S(1)} %fusion.6), channel_id=1, source_target_pairs={{0,1},{1,0},{2,3},{3,2},{4,5},{5,4},{6,7},{7,6},{8,9},{9,8},{10,11... | collective-permute-start | bytes 1572872 | tf_op jit(solution)/shard_map/ppermute | solution.py:657
  401.0 64.1 %collective-permute-start.35 = (bf16[256,1024]{1,0:T(8,128)(2,1)S(1)}, bf16[256,1024]{1,0:T(8,128)(2,1)S(1)}, u32[]{:S(2)}, u32[]{:S(2)}) collective-permute-start(bf16[256,1024]{1,0:T(8,128)(2,1)S(1)} %fusion.4), channel_id=1, source_target_pairs={{0,1},{1,0},{2,3},{3,2},{4,5},{5,4},{6,7},{7,6},{8,9},{9,8},{10,11... | collective-permute-start | bytes 1572872 | tf_op jit(solution)/shard_map/ppermute | solution.py:657
  504.4 128.5 %collective-permute-start.32 = (bf16[2048,256]{1,0:T(8,128)(2,1)S(1)}, bf16[2048,256]{1,0:T(8,128)(2,1)}, u32[]{:S(2)}, u32[]{:S(2)}) collective-permute-start(bf16[2048,256]{1,0:T(8,128)(2,1)S(1)} %copy-done.21), channel_id=1, source_target_pairs={{0,1},{1,0},{2,3},{3,2},{4,5},{5,4},{6,7},{7,6},{8,9},{9,8},{10,11... | collective-permute-start | bytes 3145736 | tf_op jit(solution)/shard_map/ppermute | solution.py:657
  512.1 120.8 %collective-permute-start.34 = (bf16[2048,256]{1,0:T(8,128)(2,1)}, bf16[2048,256]{1,0:T(8,128)(2,1)}, u32[]{:S(2)}, u32[]{:S(2)}) collective-permute-start(bf16[2048,256]{1,0:T(8,128)(2,1)} %add_convert_fusion), channel_id=1, source_target_pairs={{0,2},{1,3},{2,0},{3,1},{4,6},{5,7},{6,4},{7,5},{8,10},{9,11},{10,... | collective-permute-start | bytes 3145736 | tf_op jit(solution)/shard_map/ppermute | solution.py:657
  (91 other events, 1151.3 us)
Sparse Core Ops, SparseCore 0:
  10.6 53.4 all-gather.4
  66.7 73.2 all-gather.6
  142.6 49.2 all-gather.8
  341.8 65.9 reduce-scatter.14
  411.2 66.4 reduce-scatter.16
  481.1 66.9 reduce-scatter.18
  551.6 66.5 reduce-scatter.12
